TPU v7x, 128 devices: a whole 4x4x4 slice. The times are simulated.
128 devices in a mesh: gx: 64 (over y, x, z_lo, core), gy: 2 (over z_hi).
Axes of the slice: x: 4, y: 4, z: 4 (z_hi: 2, z_lo: 2; z = z_hi * 2 + z_lo), core: 2. Of those that a mesh axis runs over, the one named last changes fastest.
Arguments:
- field: float32 [2, 2048, 256, 128], P(None, 'gx', 'gy'), may hold values from -6 to 6
- source: float32 [2, 2048, 256, 128], P(None, 'gx', 'gy'), may hold values from -6 to 6
- wavenum_sq: float32 [2048, 256, 128], P('gx', 'gy'), may hold values from 2.47 to 4.8
- coupling_x: float32 [8, 8], replicated, may hold values from -2 to 2
- coupling_y: float32 [8, 8], replicated, may hold values from -2 to 2
Outputs:
- updated: float32 [2, 2048, 256, 128], P(None, 'gx', 'gy')
All inputs are finite; a program needn't handle non-finite values.
Results may differ from a plain program's by a relative error of at most 0.0001.
Values sent between devices are 32-bit elements; how exact they have to be, the bound alone decides.
No kernel may reach another device: no remote copies, remote signals or barrier semaphores. Data moves between devices by JAX's collectives and lax.ppermute only.
A program may use at most 128 MiB of HBM per device.

v0:
```python
import functools
import math

import jax
import jax.numpy as jnp
import ml_dtypes
import numpy as np
from jax import lax
from jax.experimental import pallas as pl
from jax.experimental.pallas import tpu as pltpu
from jax.sharding import PartitionSpec as P

RIM = 8
K0SQ = 2.4674
EPS = 2.5
CX = 32
N = 128
BF = jnp.bfloat16
F32 = jnp.float32
VMEM_LIMIT = 40 * 1024 * 1024


def two_halves(table):
    high = table.astype(ml_dtypes.bfloat16)
    low = (table - high.astype(np.float64)).astype(ml_dtypes.bfloat16)
    return np.stack([high, low])


def dft_tables():
    index = np.arange(N)
    angle = 2.0 * np.pi / N * (index[:, None] * index[None, :] % N)
    cosine, sine = np.cos(angle), np.sin(angle)
    z_forward = np.block([[cosine, -sine], [sine, cosine]])
    z_inverse = np.block([[cosine, sine], [-sine, cosine]])
    return (
        two_halves(z_forward),
        two_halves(z_inverse),
        two_halves(z_forward.T),
        two_halves(z_inverse.T),
    )


def angular_sq(length):
    freq = 2.0 * np.pi * np.fft.fftfreq(length)
    return freq * freq


def green_table():
    psq = (
        angular_sq(CX)[: CX // 2 + 1, None, None]
        + angular_sq(N)[None, :, None]
        + angular_sq(N)[None, None, :]
    )
    offset = psq - K0SQ
    denom = (offset * offset + EPS * EPS) * (CX * N * N)
    return np.stack([offset / denom, EPS / denom], axis=1).astype(np.float32)


def halves(value):
    high = value.astype(BF)
    return high, (value - high.astype(F32)).astype(BF)


def from_right(value, table):
    high, low = halves(value)
    out = jnp.dot(high, table[0], preferred_element_type=F32)
    out += jnp.dot(low, table[0], preferred_element_type=F32)
    return out + jnp.dot(high, table[1], preferred_element_type=F32)


def from_left(table, value):
    high, low = halves(value)
    out = jnp.dot(table[0], high, preferred_element_type=F32)
    out += jnp.dot(table[0], low, preferred_element_type=F32)
    return out + jnp.dot(table[1], high, preferred_element_type=F32)


def by_rows(re0, im0, re1, im1):
    return jnp.concatenate(
        [jnp.concatenate([re0, im0], axis=1), jnp.concatenate([re1, im1], axis=1)], axis=0
    )


def swap_blocks(value):
    return jnp.concatenate(
        [
            jnp.concatenate([value[:N, :N], value[N:, :N]], axis=1),
            jnp.concatenate([value[:N, N:], value[N:, N:]], axis=1),
        ],
        axis=0,
    )


def times_root(value, step, length):
    re, im = value
    step %= length
    if step == 0:
        return value
    if 4 * step == length:
        return -im, re
    if 2 * step == length:
        return -re, -im
    if 4 * step == 3 * length:
        return im, -re
    c = math.cos(2.0 * math.pi * step / length)
    s = math.sin(2.0 * math.pi * step / length)
    if 8 * step % length == 0:
        h = math.sqrt(0.5)
        sc, ss = math.copysign(1.0, c), math.copysign(1.0, s)
        first = re - im if sc == ss else re + im
        second = re + im if sc == ss else im - re
        return first * (h * sc), second * (h * sc)
    return re * c - im * s, re * s + im * c


def fft(values, sign):
    count = len(values)
    if count == 1:
        return values
    even = fft(values[0::2], sign)
    odd = fft(values[1::2], sign)
    first, second = [], []
    for k in range(count // 2):
        re, im = times_root(odd[k], sign * k, count)
        first.append((even[k][0] + re, even[k][1] + im))
        second.append((even[k][0] - re, even[k][1] - im))
    return first + second


def filter_x(load, store, green, rows):
    spectrum = fft([load(x) for x in range(CX)], -1)
    scaled = []
    for k, (re, im) in enumerate(spectrum):
        g_re = green[min(k, CX - k), 0, rows, :]
        g_im = green[min(k, CX - k), 1, rows, :]
        scaled.append((re * g_re - im * g_im, re * g_im + im * g_re))
    for x, value in enumerate(fft(scaled, 1)):
        store(x, value)


def local_kernel(
    side_ref, mix_x_ref, mix_y_ref, field_ref, source_ref, wave_ref, low_ref, high_ref, near_ref,
    z_ref, y_ref, out_ref, work_ref,
):
    block = pl.program_id(0)
    planes = field_ref.shape[1]
    for p in range(planes):
        shifted = wave_ref[p] - K0SQ
        re, im = field_ref[0, p], field_ref[1, p]
        work_ref[0, p] = shifted * re + EPS * im + source_ref[0, p]
        work_ref[1, p] = shifted * im - EPS * re + source_ref[1, p]
        for part in range(2):
            first = field_ref[part, p, 0:RIM, :]
            last = field_ref[part, p, N - RIM : N, :]
            add_low = mix_y_ref[0, 0] * last[0:1]
            add_high = mix_y_ref[1, 0] * first[0:1]
            for b in range(1, RIM):
                add_low += mix_y_ref[0, b] * last[b : b + 1]
                add_high += mix_y_ref[1, b] * first[b : b + 1]
            work_ref[part, p, 0:RIM, :] += add_low
            work_ref[part, p, N - RIM : N, :] += add_high

    def along_x(base, other_ref, weight):
        @pl.loop(0, N // 16)
        def _(t):
            rows = pl.ds(pl.multiple_of(t * 16, 16), 16)
            for part in range(2):
                source = [
                    other_ref[part, r, rows, :] - weight * near_ref[part, r, rows, :]
                    for r in range(RIM)
                ]
                for p in range(planes):
                    total = work_ref[part, p, rows, :]
                    for r in range(RIM):
                        total += mix_x_ref[base + p, r] * source[r]
                    work_ref[part, p, rows, :] = total

    low_blocks = RIM // planes

    @pl.when(block < low_blocks)
    def _():
        along_x(block * planes, high_ref, side_ref[0])

    @pl.when(block >= (CX - RIM) // planes)
    def _():
        along_x(RIM + block * planes - (CX - RIM), low_ref, side_ref[1])

    for p in range(0, planes, 2):
        wide = from_right(
            by_rows(work_ref[0, p], work_ref[1, p], work_ref[0, p + 1], work_ref[1, p + 1]), z_ref
        )
        tall = from_left(y_ref, swap_blocks(wide))
        out_ref[0, p] = tall[:N, :N]
        out_ref[1, p] = tall[N:, :N]
        out_ref[0, p + 1] = tall[:N, N:]
        out_ref[1, p + 1] = tall[N:, N:]


def side_kernel(mix_ref, face_ref, hat_ref, z_ref, table_ref, out_ref, rows_ref, wide_ref):
    @pl.loop(0, CX)
    def _(x):
        for part in range(2):
            tile = face_ref[part, x]
            total = mix_ref[0] * tile[0:1]
            for b in range(1, RIM):
                total += mix_ref[b] * tile[b : b + 1]
            rows_ref[pl.ds(pl.multiple_of(x * RIM, RIM), RIM), part * N : (part + 1) * N] = -total

    wide_ref[...] = from_right(rows_ref[...], z_ref)

    @pl.loop(0, CX // 2)
    def _(pair):
        rows = wide_ref[pl.ds(pl.multiple_of(pair * 2 * RIM, 2 * RIM), 2 * RIM), :]
        short = jnp.concatenate(
            [
                jnp.concatenate([rows[:RIM, :N], rows[RIM:, :N]], axis=1),
                jnp.concatenate([rows[:RIM, N:], rows[RIM:, N:]], axis=1),
            ],
            axis=0,
        )
        tall = from_left(table_ref, short)
        x = pair * 2
        out_ref[0, x] = hat_ref[0, x] + tall[:N, :N]
        out_ref[1, x] = hat_ref[1, x] + tall[N:, :N]
        out_ref[0, x + 1] = hat_ref[0, x + 1] + tall[:N, N:]
        out_ref[1, x + 1] = hat_ref[1, x + 1] + tall[N:, N:]


def far_kernel(
    side_ref, mix_ref, face_ref, hat_ref, z_ref, y_ref, green_ref, out_ref, work_ref
):
    @pl.loop(0, N // 16)
    def _(t):
        rows = pl.ds(pl.multiple_of(t * 16, 16), 16)
        for part in range(2):
            source = [face_ref[part, r, rows, :] for r in range(RIM)]
            for p in range(RIM):
                total = mix_ref[p, 0] * source[0]
                for r in range(1, RIM):
                    total += mix_ref[p, r] * source[r]
                work_ref[part, p, rows, :] = -total

    @pl.loop(0, RIM // 2)
    def _(pair):
        p = pair * 2
        wide = from_right(
            by_rows(work_ref[0, p], work_ref[1, p], work_ref[0, p + 1], work_ref[1, p + 1]), z_ref
        )
        tall = from_left(y_ref, swap_blocks(wide))
        work_ref[0, p] = tall[:N, :N]
        work_ref[1, p] = tall[N:, :N]
        work_ref[0, p + 1] = tall[:N, N:]
        work_ref[1, p + 1] = tall[N:, N:]

    @pl.loop(0, N // 8)
    def _(t):
        rows = pl.ds(pl.multiple_of(t * 8, 8), 8)

        def load(x):
            re, im = hat_ref[0, x, rows, :], hat_ref[1, x, rows, :]
            if x < RIM or x >= CX - RIM:
                weight = side_ref[int(x < RIM)]
                re += weight * work_ref[0, x % RIM, rows, :]
                im += weight * work_ref[1, x % RIM, rows, :]
            return re, im

        def store(x, value):
            out_ref[0, x, rows, :] = value[0]
            out_ref[1, x, rows, :] = value[1]

        filter_x(load, store, green_ref, rows)


def back_kernel(hat_ref, field_ref, wave_ref, y_ref, z_ref, out_ref):
    for p in range(0, field_ref.shape[1], 2):
        tall = jnp.concatenate(
            [
                jnp.concatenate([hat_ref[0, p], hat_ref[0, p + 1]], axis=1),
                jnp.concatenate([hat_ref[1, p], hat_ref[1, p + 1]], axis=1),
            ],
            axis=0,
        )
        wide = from_right(swap_blocks(from_left(y_ref, tall)), z_ref)
        for q in range(2):
            ratio = (wave_ref[p + q] - K0SQ) * (1.0 / EPS)
            re, im = field_ref[0, p + q], field_ref[1, p + q]
            r_re = re - wide[q * N : (q + 1) * N, :N]
            r_im = im - wide[q * N : (q + 1) * N, N:]
            out_ref[0, p + q] = re - (r_re - ratio * r_im)
            out_ref[1, p + q] = im - (r_im + ratio * r_re)


SMEM = pl.BlockSpec(memory_space=pltpu.SMEM)
WHOLE = pl.BlockSpec(memory_space=pltpu.VMEM)
VOLUME = jax.ShapeDtypeStruct((2, CX, N, N), F32)
PARAMS = pltpu.CompilerParams(vmem_limit_bytes=VMEM_LIMIT)


def cost(flops, size):
    return pl.CostEstimate(flops=flops, bytes_accessed=size, transcendentals=0)


def whole(shape):
    return pl.BlockSpec(shape, lambda i: (0,) * len(shape))


def local(side, mix_x, mix_y, field, source, wave, near, z_table, y_table):
    planes = 4
    volume = pl.BlockSpec((2, planes, N, N), lambda i: (0, i, 0, 0))
    return pl.pallas_call(
        local_kernel,
        grid=(CX // planes,),
        in_specs=[
            SMEM, SMEM, whole((2, RIM, RIM, N)), volume, volume,
            pl.BlockSpec((planes, N, N), lambda i: (i, 0, 0)),
            pl.BlockSpec((2, RIM, N, N), lambda i: (0, 0, 0, 0)),
            pl.BlockSpec((2, RIM, N, N), lambda i: (0, CX // RIM - 1, 0, 0)),
            whole((2, RIM, N, N)), whole((2, 256, 256)), whole((2, 256, 256)),
        ],
        out_specs=volume,
        out_shape=VOLUME,
        scratch_shapes=[pltpu.VMEM((2, planes, N, N), F32)],
        compiler_params=PARAMS,
        cost_estimate=cost(8 * 10**9, 14 * 2**20),
    )(side, mix_x, mix_y, field, source, wave, field, field, near, z_table, y_table)


def add_side(mix, face, hat, z_table, table):
    return pl.pallas_call(
        side_kernel,
        in_specs=[WHOLE] * 5,
        out_specs=WHOLE,
        out_shape=VOLUME,
        scratch_shapes=[pltpu.VMEM((CX * RIM, 256), F32), pltpu.VMEM((CX * RIM, 256), F32)],
        compiler_params=PARAMS,
        cost_estimate=cost(10**9, 8 * 2**20),
    )(mix, face, hat, z_table, table)


def far(side, mix, face, hat, z_table, y_table, green):
    return pl.pallas_call(
        far_kernel,
        in_specs=[SMEM, SMEM] + [WHOLE] * 5,
        out_specs=WHOLE,
        out_shape=VOLUME,
        scratch_shapes=[pltpu.VMEM((2, RIM, N, N), F32)],
        compiler_params=PARAMS,
        cost_estimate=cost(4 * 10**9, 8 * 2**20),
    )(side, mix, face, hat, z_table, y_table, green)


def back(hat, field, wave, y_table, z_table):
    planes = 4
    volume = pl.BlockSpec((2, planes, N, N), lambda i: (0, i, 0, 0))
    return pl.pallas_call(
        back_kernel,
        grid=(CX // planes,),
        in_specs=[
            volume, volume, pl.BlockSpec((planes, N, N), lambda i: (i, 0, 0)),
            whole((2, 256, 256)), whole((2, 256, 256)),
        ],
        out_specs=volume,
        out_shape=VOLUME,
        compiler_params=PARAMS,
        cost_estimate=cost(6 * 10**9, 14 * 2**20),
    )(hat, field, wave, y_table, z_table)


def body(field, source, wave, coupling_x, coupling_y):
    n_gx = lax.axis_size("gx")
    n_gy = lax.axis_size("gy")
    gx = lax.axis_index("gx")
    gy = lax.axis_index("gy")
    odd = gx % 2
    near_pairs = [(i, i ^ 1) for i in range(n_gx)]
    far_pairs = [(i, ((i + 1) ^ 1) - 1) for i in range(1, n_gx - 1)]
    side_pairs = [(i, i ^ 1) for i in range(n_gy)]

    zf, zi, yf, yi = (jnp.asarray(t) for t in dft_tables())
    green = jnp.asarray(green_table())

    mix_low, mix_high = coupling_x[:, ::-1], coupling_x[::-1, :]
    mix_x = jnp.concatenate([mix_low, mix_high], axis=0)
    mix_far = jnp.where(odd == 1, mix_high, mix_low)
    sides = jnp.stack([odd, 1 - odd]).astype(F32)
    wide_low = jnp.broadcast_to(coupling_y[:, ::-1].T[:, :, None], (RIM, RIM, N))
    wide_high = jnp.broadcast_to(coupling_y[::-1, :].T[:, :, None], (RIM, RIM, N))
    mix_y = jnp.stack([wide_low, wide_high])
    mix_side = jnp.where(gy == 1, wide_low, wide_high)

    def rim_columns(offset):
        return jnp.concatenate(
            [yf[:, :, offset : offset + RIM], yf[:, :, N + offset : N + offset + RIM]], axis=2
        )

    side_table = jnp.where(gy == 1, rim_columns(0), rim_columns(N - RIM))

    for step in range(2):
        far_out = lax.dynamic_slice_in_dim(field, odd * (CX - RIM), RIM, axis=1)
        near_out = lax.dynamic_slice_in_dim(field, (1 - odd) * (CX - RIM), RIM, axis=1)
        side_out = lax.dynamic_slice_in_dim(field, (1 - gy) * (N - RIM), RIM, axis=2)
        far_in = lax.ppermute(far_out, "gx", far_pairs)
        near_in = lax.ppermute(near_out, "gx", near_pairs)
        side_in = lax.ppermute(side_out, "gy", side_pairs)
        hat = local(sides, mix_x, mix_y, field, source, wave, near_in, zf, yf)
        hat = add_side(mix_side, side_in, hat, zf, side_table)
        hat = far(sides, mix_far, far_in, hat, zf, yf, green)
        field = back(hat, field, wave, yi, zi)
    return field


def solution(mesh):
    placed = (P(None, "gx", "gy", None), P(None, "gx", "gy", None), P("gx", "gy", None), P(), P())
    return jax.shard_map(
        body, mesh=mesh, in_specs=placed, out_specs=P(None, "gx", "gy", None), check_vma=False
    )
```

profile of v0, /device:TPU:1, one launch (start us, length us, event | category | flops | bytes accessed | tf_op | source)
XLA Modules:
  0.0 109.7 jit_solution(11254318046229510280)
XLA Ops:
  0.0 0.0 copy-start.4
  0.1 3.2 %constant_dynamic-slice_fusion.3 = (f32[2,8,128,128]{3,2,1,0:T(8,128)}, f32[2,8,128,128]{3,2,1,0:T(8,128)}) fusion(f32[2,32,128,128]{3,2,1,0:T(8,128)} %field_ref.3, s32[]{:T(128)S(6)} %select_n.50, s32[]{:T(128)S(6)} %select_n.46), kind=kLoop, calls=%fused_computation.8 | loop fusion | bytes 4194312 | tf_op jit(solution)/shard_map/dynamic_slice | solution.py:400
  3.3 1.4 %collective-permute-start.2 = (f32[2,8,128,128]{3,2,1,0:T(8,128)}, f32[2,8,128,128]{3,2,1,0:T(8,128)}, u32[]{:S(2)}, u32[]{:S(2)}) collective-permute-start(f32[2,8,128,128]{3,2,1,0:T(8,128)} %get-tuple-element.7), channel_id=1, source_target_pairs={{0,2},{2,0},{4,6},{6,4},{8,10},{10,8},{12,14},{14,12},{16,18},{18,... | collective-permute-start | bytes 3145736 | tf_op jit(solution)/shard_map/ppermute | solution.py:403
  4.7 1.0 constant_dynamic-slice_fusion.4
  5.7 3.8 %collective-permute-start.1 = (f32[2,32,8,128]{3,2,1,0:T(8,128)S(1)}, f32[2,32,8,128]{3,2,1,0:T(8,128)S(1)}, u32[]{:S(2)}, u32[]{:S(2)}) collective-permute-start(f32[2,32,8,128]{3,2,1,0:T(8,128)S(1)} %constant_dynamic-slice_fusion.4), channel_id=1, source_target_pairs={{0,1},{1,0},{2,3},{3,2},{4,5},{5,4},{6,7},{7,6},{8,9},{9,8},{10,11... | collective-permute-start | bytes 786440 | tf_op jit(solution)/shard_map/ppermute | solution.py:404
  9.5 2.8 %collective-permute-start = (f32[2,8,128,128]{3,2,1,0:T(8,128)}, f32[2,8,128,128]{3,2,1,0:T(8,128)}, u32[]{:S(2)}, u32[]{:S(2)}) collective-permute-start(f32[2,8,128,128]{3,2,1,0:T(8,128)} %get-tuple-element.8), channel_id=1, source_target_pairs={{2,4},{4,2},{6,8},{8,6},{10,12},{12,10},{14,16},{16,14},{18,20},{2... | collective-permute-start | bytes 3145736 | tf_op jit(solution)/shard_map/ppermute | solution.py:402
  12.3 0.1 rev.13
  12.4 0.1 rev.14
  12.5 0.1 copy.12
  12.5 0.1 copy.11
  12.6 0.1 copy.13
  12.7 0.1 add_convert_fusion.side_ref
  12.8 0.1 stack_broadcast_in_dim.5
  12.8 0.1 stack_broadcast_in_dim.4
  13.0 0.0 collective-permute-done.2.near_ref
  13.0 0.0 copy-start
  13.0 2.2 %copy-done = f32[2,32,128,128]{3,2,1,0:T(8,128)S(1)} copy-done((f32[2,32,128,128]{3,2,1,0:T(8,128)S(1)}, f32[2,32,128,128]{3,2,1,0:T(8,128)}, u32[]{:S(2)}) %copy-start) | copy-done | bytes 4194328
  15.2 12.5 %shard_map.100.hat_ref = f32[2,32,128,128]{3,2,1,0:T(8,128)S(1)} custom-call(f32[2]{0:T(128)S(1)} %add_convert_fusion.side_ref, f32[16,8]{1,0:T(8,128)S(1)} %pad_maximum_fusion.1.mix_x_ref, f32[2,8,8,128]{3,2,1,0:T(8,128)S(1)} %pad_maximum_fusion.mix_y_ref, f32[2,32,128,128]{3,2,1,0:T(8,128)S(1)} %copy-done, f32[2,32,128,128]{3,2,1,0:T(8,128)} %source_ref.3, ...), custom_call_target="tpu_custom_call" | custom-call | flops 8000000000 | bytes 14680064 | tf_op jit(solution)/shard_map/pallas_call | solution.py:310
  27.7 0.1 broadcast_in_dim.2.mix_ref
  27.8 4.5 %shard_map.101.hat_ref = f32[2,32,128,128]{3,2,1,0:T(8,128)S(1)} custom-call(f32[8,8,128]{2,1,0:T(8,128)S(1)} %broadcast_in_dim.2.mix_ref, f32[2,32,8,128]{3,2,1,0:T(8,128)S(1)} %collective-permute-done.1.face_ref, f32[2,32,128,128]{3,2,1,0:T(8,128)S(1)} %shard_map.100.hat_ref, bf16[2,256,256]{2,1,0:T(8,128)(2,1)S(1)} %copy-done.1, ...), custom_call_target="tpu_custom_call" | custom-call | flops 1000000000 | bytes 8388608 | tf_op jit(solution)/shard_map/pallas_call | solution.py:329
  32.3 5.9 %collective-permute-done.face_ref = f32[2,8,128,128]{3,2,1,0:T(8,128)} collective-permute-done((f32[2,8,128,128]{3,2,1,0:T(8,128)}, f32[2,8,128,128]{3,2,1,0:T(8,128)}, u32[]{:S(2)}, u32[]{:S(2)}) %collective-permute-start) | collective-permute-done | bytes 1048608 | tf_op jit(solution)/shard_map/ppermute | solution.py:402
  38.2 8.3 %shard_map.102.hat_ref = f32[2,32,128,128]{3,2,1,0:T(8,128)S(1)} custom-call(f32[2]{0:T(128)S(1)} %add_convert_fusion.side_ref, f32[8,8]{1,0:T(8,128)S(1)} %broadcast_select_fusion.2.mix_ref, f32[2,8,128,128]{3,2,1,0:T(8,128)} %collective-permute-done.face_ref, f32[2,32,128,128]{3,2,1,0:T(8,128)S(1)} %shard_map.101.hat_ref, ...), custom_call_target="tpu_custom_call" | custom-call | flops 4000000000 | bytes 8388608 | tf_op jit(solution)/shard_map/pallas_call | solution.py:341
  46.4 8.9 %shard_map.103.field_ref.low_ref.high_ref = f32[2,32,128,128]{3,2,1,0:T(8,128)S(1)} custom-call(f32[2,32,128,128]{3,2,1,0:T(8,128)S(1)} %shard_map.102.hat_ref, f32[2,32,128,128]{3,2,1,0:T(8,128)} %field_ref.3, f32[32,128,128]{2,1,0:T(8,128)S(1)} %copy-done.2, bf16[2,256,256]{2,1,0:T(8,128)(2,1)S(1)} %copy-done.1, bf16[2,256,256]{2,1,0:T(8,128)(2,1)S(1)} %copy-done.4), custom_call_target="tpu_custom_call" | custom-call | flops 6000000000 | bytes 14680064 | tf_op jit(solution)/shard_map/pallas_call | solution.py:355
  55.4 0.2 constant_dynamic-slice_fusion
  55.6 0.1 collective-permute-start.5
  55.7 4.4 %collective-permute-start.3 = (f32[2,8,128,128]{3,2,1,0:T(8,128)S(1)}, f32[2,8,128,128]{3,2,1,0:T(8,128)S(1)}, u32[]{:S(2)}, u32[]{:S(2)}) collective-permute-start(f32[2,8,128,128]{3,2,1,0:T(8,128)S(1)} %get-tuple-element.6), channel_id=1, source_target_pairs={{2,4},{4,2},{6,8},{8,6},{10,12},{12,10},{14,16},{16,14},{18,20},{2... | collective-permute-start | bytes 3145736 | tf_op jit(solution)/shard_map/ppermute | solution.py:402
  60.1 0.1 collective-permute-start.4
  60.2 12.1 %shard_map.104.hat_ref = f32[2,32,128,128]{3,2,1,0:T(8,128)S(1)} custom-call(f32[2]{0:T(128)S(1)} %add_convert_fusion.side_ref, f32[16,8]{1,0:T(8,128)S(1)} %pad_maximum_fusion.1.mix_x_ref, f32[2,8,8,128]{3,2,1,0:T(8,128)S(1)} %pad_maximum_fusion.mix_y_ref, f32[2,32,128,128]{3,2,1,0:T(8,128)S(1)} %shard_map.103.field_ref.low_ref.high_ref, ...), custom_call_target="tpu_custom_call" | custom-call | flops 8000000000 | bytes 14680064 | tf_op jit(solution)/shard_map/pallas_call | solution.py:310
  72.4 16.7 %collective-permute-done.4.face_ref = f32[2,32,8,128]{3,2,1,0:T(8,128)S(1)} collective-permute-done((f32[2,32,8,128]{3,2,1,0:T(8,128)S(1)}, f32[2,32,8,128]{3,2,1,0:T(8,128)S(1)}, u32[]{:S(2)}, u32[]{:S(2)}) %collective-permute-start.4) | collective-permute-done | bytes 262176 | tf_op jit(solution)/shard_map/ppermute | solution.py:404
  89.1 4.5 %shard_map.105.hat_ref = f32[2,32,128,128]{3,2,1,0:T(8,128)S(1)} custom-call(f32[8,8,128]{2,1,0:T(8,128)S(1)} %broadcast_in_dim.2.mix_ref, f32[2,32,8,128]{3,2,1,0:T(8,128)S(1)} %collective-permute-done.4.face_ref, f32[2,32,128,128]{3,2,1,0:T(8,128)S(1)} %shard_map.104.hat_ref, bf16[2,256,256]{2,1,0:T(8,128)(2,1)S(1)} %copy-done.1, ...), custom_call_target="tpu_custom_call" | custom-call | flops 1000000000 | bytes 8388608 | tf_op jit(solution)/shard_map/pallas_call | solution.py:329
  93.6 7.6 %shard_map.106.hat_ref = f32[2,32,128,128]{3,2,1,0:T(8,128)S(1)} custom-call(f32[2]{0:T(128)S(1)} %add_convert_fusion.side_ref, f32[8,8]{1,0:T(8,128)S(1)} %broadcast_select_fusion.2.mix_ref, f32[2,8,128,128]{3,2,1,0:T(8,128)S(1)} %collective-permute-done.3.face_ref, f32[2,32,128,128]{3,2,1,0:T(8,128)S(1)} %shard_map.105.hat_ref, ...), custom_call_target="tpu_custom_call" | custom-call | flops 4000000000 | bytes 8388608 | tf_op jit(solution)/shard_map/pallas_call | solution.py:341
  101.3 8.4 %shard_map.107 = f32[2,32,128,128]{3,2,1,0:T(8,128)} custom-call(f32[2,32,128,128]{3,2,1,0:T(8,128)S(1)} %shard_map.106.hat_ref, f32[2,32,128,128]{3,2,1,0:T(8,128)S(1)} %shard_map.103.field_ref.low_ref.high_ref, f32[32,128,128]{2,1,0:T(8,128)S(1)} %copy-done.2, bf16[2,256,256]{2,1,0:T(8,128)(2,1)S(1)} %copy-done.1, bf16[2,256,256]{2,1,0:T(8,128)(2,1)S(1)} %copy-done.4), custom_call_target="tpu_custom_call" | custom-call | flops 6000000000 | bytes 14680064 | tf_op jit(solution)/shard_map/pallas_call | solution.py:355
  (26 shorter events, 0.1 us)
Async XLA Ops:
  0.0 12.9 %copy-start.5 = (bf16[2,256,16]{2,1,0:T(8,128)(2,1)S(1)}, bf16[2,256,16]{2,1,0:T(8,128)(2,1)}, u32[]{:S(2)}) copy-start(bf16[2,256,16]{2,1,0:T(8,128)(2,1)} %constant.48) | copy-start | bytes 49156
  0.0 12.9 %copy-start.6 = (bf16[2,256,16]{2,1,0:T(8,128)(2,1)S(1)}, bf16[2,256,16]{2,1,0:T(8,128)(2,1)}, u32[]{:S(2)}) copy-start(bf16[2,256,16]{2,1,0:T(8,128)(2,1)} %constant.45) | copy-start | bytes 49156
  0.0 13.0 %copy-start.1 = (bf16[2,256,256]{2,1,0:T(8,128)(2,1)S(1)}, bf16[2,256,256]{2,1,0:T(8,128)(2,1)}, u32[]{:S(2)}) copy-start(bf16[2,256,256]{2,1,0:T(8,128)(2,1)} %constant.37.clone.z_ref.y_ref) | copy-start | bytes 786436
  0.0 13.0 %copy-start.4 = (bf16[2,256,256]{2,1,0:T(8,128)(2,1)S(1)}, bf16[2,256,256]{2,1,0:T(8,128)(2,1)}, u32[]{:S(2)}) copy-start(bf16[2,256,256]{2,1,0:T(8,128)(2,1)} %constant.38.clone.y_ref.z_ref) | copy-start | bytes 786436
  0.0 12.3 %copy-start.7 = (f32[8,8]{1,0:T(8,128)S(1)}, f32[8,8]{1,0:T(8,128)}, u32[]{:S(2)}) copy-start(f32[8,8]{1,0:T(8,128)} %param.13) | copy-start | bytes 772
  0.0 12.4 %copy-start.8 = (f32[8,8]{1,0:T(8,128)S(1)}, f32[8,8]{1,0:T(8,128)}, u32[]{:S(2)}) copy-start(f32[8,8]{1,0:T(8,128)} %param.14) | copy-start | bytes 772
  0.0 13.0 %copy-start.2 = (f32[32,128,128]{2,1,0:T(8,128)S(1)}, f32[32,128,128]{2,1,0:T(8,128)}, u32[]{:S(2)}) copy-start(f32[32,128,128]{2,1,0:T(8,128)} %wave_ref.7) | copy-start | bytes 6291460
  3.3 9.7 %collective-permute-start.2 = (f32[2,8,128,128]{3,2,1,0:T(8,128)}, f32[2,8,128,128]{3,2,1,0:T(8,128)}, u32[]{:S(2)}, u32[]{:S(2)}) collective-permute-start(f32[2,8,128,128]{3,2,1,0:T(8,128)} %get-tuple-element.7), channel_id=1, source_target_pairs={{0,2},{2,0},{4,6},{6,4},{8,10},{10,8},{12,14},{14,12},{16,18},{18,... | collective-permute-start | bytes 3145736 | tf_op jit(solution)/shard_map/ppermute | solution.py:403
  5.7 22.0 %collective-permute-start.1 = (f32[2,32,8,128]{3,2,1,0:T(8,128)S(1)}, f32[2,32,8,128]{3,2,1,0:T(8,128)S(1)}, u32[]{:S(2)}, u32[]{:S(2)}) collective-permute-start(f32[2,32,8,128]{3,2,1,0:T(8,128)S(1)} %constant_dynamic-slice_fusion.4), channel_id=1, source_target_pairs={{0,1},{1,0},{2,3},{3,2},{4,5},{5,4},{6,7},{7,6},{8,9},{9,8},{10,11... | collective-permute-start | bytes 786440 | tf_op jit(solution)/shard_map/ppermute | solution.py:404
  9.5 28.7 %collective-permute-start = (f32[2,8,128,128]{3,2,1,0:T(8,128)}, f32[2,8,128,128]{3,2,1,0:T(8,128)}, u32[]{:S(2)}, u32[]{:S(2)}) collective-permute-start(f32[2,8,128,128]{3,2,1,0:T(8,128)} %get-tuple-element.8), channel_id=1, source_target_pairs={{2,4},{4,2},{6,8},{8,6},{10,12},{12,10},{14,16},{16,14},{18,20},{2... | collective-permute-start | bytes 3145736 | tf_op jit(solution)/shard_map/ppermute | solution.py:402
  13.0 2.2 %copy-start = (f32[2,32,128,128]{3,2,1,0:T(8,128)S(1)}, f32[2,32,128,128]{3,2,1,0:T(8,128)}, u32[]{:S(2)}) copy-start(f32[2,32,128,128]{3,2,1,0:T(8,128)} %field_ref.3) | copy-start | bytes 12582916
  27.8 10.4 %copy-start.3 = (f32[17,2,128,128]{3,2,1,0:T(8,128)S(1)}, f32[17,2,128,128]{3,2,1,0:T(8,128)}, u32[]{:S(2)}) copy-start(f32[17,2,128,128]{3,2,1,0:T(8,128)} %constant.39.clone.green_ref) | copy-start | bytes 6684676
  55.6 4.6 %collective-permute-start.5 = (f32[2,8,128,128]{3,2,1,0:T(8,128)S(1)}, f32[2,8,128,128]{3,2,1,0:T(8,128)S(1)}, u32[]{:S(2)}, u32[]{:S(2)}) collective-permute-start(f32[2,8,128,128]{3,2,1,0:T(8,128)S(1)} %get-tuple-element.5), channel_id=1, source_target_pairs={{0,2},{2,0},{4,6},{6,4},{8,10},{10,8},{12,14},{14,12},{16,18},{18,... | collective-permute-start | bytes 3145736 | tf_op jit(solution)/shard_map/ppermute | solution.py:403
  55.7 37.9 %collective-permute-start.3 = (f32[2,8,128,128]{3,2,1,0:T(8,128)S(1)}, f32[2,8,128,128]{3,2,1,0:T(8,128)S(1)}, u32[]{:S(2)}, u32[]{:S(2)}) collective-permute-start(f32[2,8,128,128]{3,2,1,0:T(8,128)S(1)} %get-tuple-element.6), channel_id=1, source_target_pairs={{2,4},{4,2},{6,8},{8,6},{10,12},{12,10},{14,16},{16,14},{18,20},{2... | collective-permute-start | bytes 3145736 | tf_op jit(solution)/shard_map/ppermute | solution.py:402
  60.1 29.0 %collective-permute-start.4 = (f32[2,32,8,128]{3,2,1,0:T(8,128)S(1)}, f32[2,32,8,128]{3,2,1,0:T(8,128)S(1)}, u32[]{:S(2)}, u32[]{:S(2)}) collective-permute-start(f32[2,32,8,128]{3,2,1,0:T(8,128)S(1)} %constant_dynamic-slice_fusion.1), channel_id=1, source_target_pairs={{0,1},{1,0},{2,3},{3,2},{4,5},{5,4},{6,7},{7,6},{8,9},{9,8},{10,11... | collective-permute-start | bytes 786440 | tf_op jit(solution)/shard_map/ppermute | solution.py:404
where the time goes:
time: 110 us
  Pallas kernels  66.8 us (61%)
  waiting for transfers between devices  22.6 us (21%)
  starting transfers between devices  12.5 us (11%)
  local copies, waits for them, and re-layouts  7.28 us (7%)
    pallas_call x2, Pallas kernels, local(): pl.pallas_call(local_kernel, grid=(CX // planes,), in_specs=[SMEM, SMEM,...  24.6 us
    pallas_call x2, Pallas kernels, back(): pl.pallas_call(back_kernel, grid=(CX // planes,), in_specs=[volume, volum...  17.3 us
    ppermute x2, waiting for transfers between devices, body(): side_in = lax.ppermute(side_out, 'gy', side_pairs)  16.7 us
    pallas_call x2, Pallas kernels, far(): pl.pallas_call(far_kernel, in_specs=[SMEM, SMEM] + [WHOLE] * 5, out_specs...  15.9 us
    pallas_call x2, Pallas kernels, add_side(): pl.pallas_call(side_kernel, in_specs=[WHOLE] * 5, out_specs=WHOLE, out_sh...  9.03 us
    ppermute x2, starting transfers between devices, body(): far_in = lax.ppermute(far_out, 'gx', far_pairs)  7.19 us
    ppermute x2, waiting for transfers between devices, body(): far_in = lax.ppermute(far_out, 'gx', far_pairs)  5.89 us
    ppermute x2, starting transfers between devices, body(): side_in = lax.ppermute(side_out, 'gy', side_pairs)  3.87 us
  transfers between devices with their start and end apart: 6, of which 2 were waited for; matrix products, arithmetic and copies ran while one was open for 2% of the time, Pallas kernels for 31%

commit v1 on v0

v1 whole, which is shorter than its diff:
```python
import functools
import math

import jax
import jax.numpy as jnp
import ml_dtypes
import numpy as np
from jax import lax
from jax.experimental import pallas as pl
from jax.experimental.pallas import tpu as pltpu
from jax.sharding import PartitionSpec as P

RIM = 8
HALF = 4
K0SQ = 2.4674
EPS = 2.5
CX = 32
N = 128
BF = jnp.bfloat16
F32 = jnp.float32
VMEM_LIMIT = 24 * 1024 * 1024


def two_halves(table):
    high = table.astype(ml_dtypes.bfloat16)
    low = (table - high.astype(np.float64)).astype(ml_dtypes.bfloat16)
    return np.stack([high, low])


def dft_tables():
    index = np.arange(N)
    angle = 2.0 * np.pi / N * (index[:, None] * index[None, :] % N)
    cosine, sine = np.cos(angle), np.sin(angle)
    z_forward = np.block([[cosine, -sine], [sine, cosine]])
    z_inverse = np.block([[cosine, sine], [-sine, cosine]])
    return (
        two_halves(z_forward),
        two_halves(z_inverse),
        two_halves(z_forward.T),
        two_halves(z_inverse.T),
    )


def side_tables(table):
    table = table.reshape(2, 2 * N, 2, N)
    return np.stack(
        [
            table[:, :, :, rows].reshape(2, 2 * N, 2 * RIM)
            for rows in (slice(0, RIM), slice(N - RIM, N))
        ]
    )


def angular_sq(length):
    freq = 2.0 * np.pi * np.fft.fftfreq(length)
    return freq * freq


def green_lines():
    table = green_table().astype(np.float64)
    both = np.concatenate([table, table[-2:0:-1]])
    lines = CX * np.fft.ifft(both[:, 0] + 1j * both[:, 1], axis=0)[:RIM]
    return np.stack([lines.real, lines.imag], axis=1).astype(np.float32)


def green_table():
    psq = (
        angular_sq(CX)[: CX // 2 + 1, None, None]
        + angular_sq(N)[None, :, None]
        + angular_sq(N)[None, None, :]
    )
    offset = psq - K0SQ
    denom = (offset * offset + EPS * EPS) * (CX * N * N)
    return np.stack([offset / denom, EPS / denom], axis=1).astype(np.float32)


def halves(value):
    high = value.astype(BF)
    return high, (value - high.astype(F32)).astype(BF)


def from_right(value, table):
    high, low = halves(value)
    out = jnp.dot(high, table[0], preferred_element_type=F32)
    out += jnp.dot(low, table[0], preferred_element_type=F32)
    return out + jnp.dot(high, table[1], preferred_element_type=F32)


def from_left(table, value):
    high, low = halves(value)
    out = jnp.dot(table[0], high, preferred_element_type=F32)
    out += jnp.dot(table[0], low, preferred_element_type=F32)
    return out + jnp.dot(table[1], high, preferred_element_type=F32)


def z_product(planes, table):
    count = planes[0][0].shape[0]
    tall = jnp.concatenate([jnp.concatenate([re, im], axis=1) for re, im in planes], axis=0)
    out = from_right(tall, table)
    parts = [out[k * count : (k + 1) * count] for k in range(len(planes))]
    return [(part[:, :N], part[:, N:]) for part in parts]


def y_product(planes, table):
    wide = jnp.concatenate(
        [jnp.concatenate([plane[part] for plane in planes], axis=1) for part in range(2)], axis=0
    )
    out = from_left(table, wide)
    parts = [out[:, k * N : (k + 1) * N] for k in range(len(planes))]
    return [(part[:N], part[N:]) for part in parts]


def transform(product, table, ref, count, group):
    def one(first):
        planes = [(ref[0, first + k], ref[1, first + k]) for k in range(group)]
        for k, (re, im) in enumerate(product(planes, table)):
            ref[0, first + k] = re
            ref[1, first + k] = im

    if count == group:
        one(0)
    else:
        pl.loop(0, count // group)(lambda i: one(i * group))


def times_root(value, step, length):
    re, im = value
    step %= length
    if step == 0:
        return value
    if 4 * step == length:
        return -im, re
    if 2 * step == length:
        return -re, -im
    if 4 * step == 3 * length:
        return im, -re
    c = math.cos(2.0 * math.pi * step / length)
    s = math.sin(2.0 * math.pi * step / length)
    if 8 * step % length == 0:
        h = math.sqrt(0.5)
        sc, ss = math.copysign(1.0, c), math.copysign(1.0, s)
        first = re - im if sc == ss else re + im
        second = re + im if sc == ss else im - re
        return first * (h * sc), second * (h * sc)
    return re * c - im * s, re * s + im * c


def fft(values, sign):
    count = len(values)
    if count == 1:
        return values
    even = fft(values[0::2], sign)
    odd = fft(values[1::2], sign)
    first, second = [], []
    for k in range(count // 2):
        re, im = times_root(odd[k], sign * k, count)
        first.append((even[k][0] + re, even[k][1] + im))
        second.append((even[k][0] - re, even[k][1] - im))
    return first + second


def fft_of_first(values, count):
    given = len(values)
    ratio = count // given
    out = [None] * count
    for k in range(ratio):
        turned = [times_root(value, -n * k, count) for n, value in enumerate(values)]
        out[k::ratio] = fft(turned, -1)
    return out


def filtered(spectrum, green, rows):
    scaled = []
    for k, (re, im) in enumerate(spectrum):
        g_re = green[min(k, CX - k), 0, rows, :]
        g_im = green[min(k, CX - k), 1, rows, :]
        scaled.append((re * g_re - im * g_im, re * g_im + im * g_re))
    return fft(scaled, 1)


def tiles(count, size):
    def wrap(step):
        pl.loop(0, count // size)(lambda t: step(pl.ds(pl.multiple_of(t * size, size), size)))

    return wrap


def mixed(mix_ref, row, first, source):
    total = mix_ref[row, first] * source[0]
    for r in range(1, len(source)):
        total += mix_ref[row, first + r] * source[r]
    return total


def cut_kernel(place_ref, field_ref, side_ref, first_ref, near_ref, second_ref, sems):
    far, near, rows = place_ref[0], place_ref[1], place_ref[2]
    rows = pl.multiple_of(rows, RIM)
    copies = [
        pltpu.make_async_copy(field_ref.at[:, :, pl.ds(rows, RIM), :], side_ref, sems.at[0]),
        pltpu.make_async_copy(field_ref.at[:, pl.ds(far, HALF)], first_ref, sems.at[1]),
        pltpu.make_async_copy(field_ref.at[:, pl.ds(far + HALF, HALF)], second_ref, sems.at[2]),
        pltpu.make_async_copy(field_ref.at[:, pl.ds(near, RIM)], near_ref, sems.at[3]),
    ]
    for copy in copies:
        copy.start()
    for copy in copies:
        copy.wait()


def by_depth(coupling_ref, side, b):
    rows = lax.broadcasted_iota(jnp.int32, (RIM, N), 0)
    column = jnp.zeros((RIM, N), F32)
    for a in range(RIM):
        value = coupling_ref[a, RIM - 1 - b] if side == 0 else coupling_ref[RIM - 1 - a, b]
        column = jnp.where(rows == a, value, column)
    return column


def spectrum_kernel(
    place_ref, x_ref, y_coupling_ref, planes_ref, z_ref, y_ref, mix_x_ref, mix_far_ref, mix_y_ref, out_ref
):
    odd = place_ref[0] > 0
    for a in range(RIM):
        for b in range(RIM):
            low, high = x_ref[a, RIM - 1 - b], x_ref[RIM - 1 - a, b]
            mix_x_ref[a, b] = low
            mix_x_ref[RIM + a, b] = high
            mix_far_ref[a, b] = jnp.where(odd, high, low)
    for side in range(2):
        for b in range(RIM):
            mix_y_ref[side, b] = by_depth(y_coupling_ref, side, b)
    planes = [(planes_ref[0, k], planes_ref[1, k]) for k in range(HALF)]
    for k, (re, im) in enumerate(y_product(z_product(planes, z_ref), y_ref)):
        out_ref[0, k] = re
        out_ref[1, k] = im


def local_kernel(
    side_ref, mix_x_ref, mix_y_ref, field_ref, source_ref, wave_ref, near_ref, z_ref, y_ref, after_ref,
    out_ref,
):
    @pl.loop(0, CX)
    def _(x):
        shifted = wave_ref[x] - K0SQ
        re, im = field_ref[0, x], field_ref[1, x]
        out_ref[0, x] = shifted * re + EPS * im + source_ref[0, x]
        out_ref[1, x] = shifted * im - EPS * re + source_ref[1, x]
        for part in range(2):
            first = field_ref[part, x, 0:RIM, :]
            last = field_ref[part, x, N - RIM : N, :]
            add_low = mix_y_ref[0, 0] * last[0:1]
            add_high = mix_y_ref[1, 0] * first[0:1]
            for b in range(1, RIM):
                add_low += mix_y_ref[0, b] * last[b : b + 1]
                add_high += mix_y_ref[1, b] * first[b : b + 1]
            out_ref[part, x, 0:RIM, :] += add_low
            out_ref[part, x, N - RIM : N, :] += add_high

    for side, base, other in ((0, 0, CX - RIM), (1, CX - RIM, 0)):
        weight = side_ref[side]

        @tiles(N, 16)
        def _(rows):
            for part in range(2):
                source = [
                    field_ref[part, other + r, rows, :] - weight * near_ref[part, r, rows, :]
                    for r in range(RIM)
                ]
                for p in range(RIM):
                    out_ref[part, base + p, rows, :] += mixed(mix_x_ref, side * RIM + p, 0, source)

    transform(z_product, z_ref, out_ref, CX, 16)
    transform(y_product, y_ref, out_ref, CX, 16)


def side_kernel(
    place_ref, mix_y_ref, face_ref, hat_ref, z_ref, table_ref, green_ref, out_ref, rows_ref, wide_ref
):
    upper = place_ref[3]
    mix_ref, table_ref = mix_y_ref.at[upper], table_ref.at[upper]

    @pl.loop(0, CX)
    def _(x):
        for part in range(2):
            tile = face_ref[part, x]
            total = mix_ref[0] * tile[0:1]
            for b in range(1, RIM):
                total += mix_ref[b] * tile[b : b + 1]
            rows_ref[pl.ds(pl.multiple_of(x * RIM, RIM), RIM), part * N : (part + 1) * N] = -total

    wide_ref[...] = from_right(rows_ref[...], z_ref)

    group = 8

    @pl.loop(0, CX // group)
    def _(i):
        rows = wide_ref[pl.ds(pl.multiple_of(i * group * RIM, group * RIM), group * RIM), :]
        parts = [rows[k * RIM : (k + 1) * RIM] for k in range(group)]
        short = [(part[:, :N], part[:, N:]) for part in parts]
        for k, (re, im) in enumerate(y_product(short, table_ref)):
            x = i * group + k
            out_ref[0, x] = hat_ref[0, x] + re
            out_ref[1, x] = hat_ref[1, x] + im

    @tiles(N, 8)
    def _(rows):
        given = [(out_ref[0, x, rows, :], out_ref[1, x, rows, :]) for x in range(CX)]
        for x, (re, im) in enumerate(filtered(fft(given, -1), green_ref, rows)):
            out_ref[0, x, rows, :] = re
            out_ref[1, x, rows, :] = im


def first_kernel(mix_ref, face_ref, z_ref, y_ref, after_ref, out_ref):
    @tiles(N, 16)
    def _(rows):
        for part in range(2):
            source = [face_ref[part, r, rows, :] for r in range(HALF)]
            for p in range(RIM):
                out_ref[part, p, rows, :] = -mixed(mix_ref, p, 0, source)

    transform(z_product, z_ref, out_ref, RIM, RIM)
    transform(y_product, y_ref, out_ref, RIM, RIM)


def damped(re, im, back, wave):
    ratio = (wave - K0SQ) * (1.0 / EPS)
    r_re, r_im = re - back[0], im - back[1]
    return re - (r_re - ratio * r_im), im - (r_im + ratio * r_re)


def early_kernel(
    place_ref, mix_ref, second_ref, first_ref, part_ref, line_ref, field_ref, wave_ref, y_ref, z_ref,
    hat_ref, out_ref, work_ref,
):
    base = place_ref[0]

    @tiles(N, 8)
    def _(rows):
        for part in range(2):
            source = [second_ref[part, r, rows, :] for r in range(HALF)]
            for p in range(RIM):
                hat_ref[part, p, rows, :] = first_ref[part, p, rows, :] - mixed(
                    mix_ref, p, HALF, source
                )

    @tiles(N, 8)
    def _(rows):
        given = [(hat_ref[0, p, rows, :], hat_ref[1, p, rows, :]) for p in range(RIM)]
        lines = [(line_ref[d, 0, rows, :], line_ref[d, 1, rows, :]) for d in range(RIM)]
        for p in range(HALF):
            re = part_ref[0, base + p, rows, :]
            im = part_ref[1, base + p, rows, :]
            for q, (t_re, t_im) in enumerate(given):
                g_re, g_im = lines[abs(p - q)]
                re += t_re * g_re - t_im * g_im
                im += t_re * g_im + t_im * g_re
            work_ref[0, p, rows, :] = re
            work_ref[1, p, rows, :] = im

    planes = [(work_ref[0, k], work_ref[1, k]) for k in range(HALF)]
    for k, back in enumerate(z_product(y_product(planes, y_ref), z_ref)):
        re, im = damped(field_ref[0, base + k], field_ref[1, base + k], back, wave_ref[base + k])
        out_ref[0, k] = re
        out_ref[1, k] = im


def filter_far(base, given_of, part_ref, green_ref, work_ref):
    @tiles(N, 8)
    def _(rows):
        spectrum = fft_of_first(given_of(rows), CX)
        for k, (re, im) in enumerate(filtered(spectrum, green_ref, rows)):
            x = lax.rem(base + k, CX)
            work_ref[0, x, rows, :] = part_ref[0, x, rows, :] + re
            work_ref[1, x, rows, :] = part_ref[1, x, rows, :] + im


def step_back(work_ref, field_ref, wave_ref, y_ref, z_ref, out_ref):
    group = 16
    transform(y_product, y_ref, work_ref, CX, group)

    @pl.loop(0, CX // group)
    def _(i):
        first = i * group
        planes = [(work_ref[0, first + k], work_ref[1, first + k]) for k in range(group)]
        for k, back in enumerate(z_product(planes, z_ref)):
            x = first + k
            re, im = damped(field_ref[0, x], field_ref[1, x], back, wave_ref[x])
            out_ref[0, x] = re
            out_ref[1, x] = im


def middle_kernel(
    place_ref, hat_ref, part_ref, green_ref, field_ref, wave_ref, yi_ref, zi_ref, z_ref, y_ref,
    out_ref, side_ref, near_ref, second_ref, work_ref,
):
    base = place_ref[0]

    def given_of(rows):
        return [(hat_ref[0, p, rows, :], hat_ref[1, p, rows, :]) for p in range(RIM)]

    filter_far(base, given_of, part_ref, green_ref, work_ref)
    step_back(work_ref, field_ref, wave_ref, yi_ref, zi_ref, out_ref)

    cut = pl.ds(pl.multiple_of(place_ref[2], RIM), RIM)
    for part in range(2):
        side_ref[part] = out_ref[part, :, cut, :]
        near_ref[part] = out_ref[part, pl.ds(place_ref[1], RIM)]
    planes = [(out_ref[0, base + k], out_ref[1, base + k]) for k in range(HALF, RIM)]
    for k, (re, im) in enumerate(y_product(z_product(planes, z_ref), y_ref)):
        second_ref[0, k] = re
        second_ref[1, k] = im


def last_kernel(
    place_ref, mix_ref, second_ref, first_ref, part_ref, green_ref, field_ref, wave_ref, yi_ref, zi_ref,
    out_ref, work_ref, done_ref, sems,
):
    def given_of(rows):
        sums = []
        for part in range(2):
            source = [second_ref[part, r, rows, :] for r in range(HALF)]
            sums.append(
                [
                    first_ref[part, p, rows, :] - mixed(mix_ref, p, HALF, source)
                    for p in range(RIM)
                ]
            )
        return list(zip(*sums))

    filter_far(place_ref[0], given_of, part_ref, green_ref, work_ref)
    transform(y_product, yi_ref, work_ref, CX, 16)
    copies = []
    for i, (first, group) in enumerate(((0, 16), (16, 8), (24, 8))):
        planes = [(work_ref[0, first + k], work_ref[1, first + k]) for k in range(group)]
        for k, back in enumerate(z_product(planes, zi_ref)):
            x = first + k
            re, im = damped(field_ref[0, x], field_ref[1, x], back, wave_ref[x])
            done_ref[0, x] = re
            done_ref[1, x] = im
        span = pl.ds(first, group)
        copies.append(pltpu.make_async_copy(done_ref.at[:, span], out_ref.at[:, span], sems.at[i]))
        copies[-1].start()
    for copy in copies:
        copy.wait()


SMEM = pl.BlockSpec(memory_space=pltpu.SMEM)
WHOLE = pl.BlockSpec(memory_space=pltpu.VMEM)


def array(*shape):
    return jax.ShapeDtypeStruct(shape, F32)


VOLUME = array(2, CX, N, N)
FACE = array(2, RIM, N, N)
PART = array(2, HALF, N, N)
SIDE = array(2, CX, RIM, N)


PARAMS = pltpu.CompilerParams(vmem_limit_bytes=VMEM_LIMIT)


def cost(weight):
    return pl.CostEstimate(flops=weight * 10**9, bytes_accessed=weight * 10**6, transcendentals=0)


COST = cost(1)


def call(kernel, scalars, operands, out, scratch=(), after=None, weight=1):
    later = [] if after is None else [after]
    return pl.pallas_call(
        kernel,
        in_specs=[SMEM] * len(scalars) + [WHOLE] * len(operands)
        + [pl.BlockSpec(memory_space=pl.ANY)] * len(later),
        out_specs=jax.tree.map(lambda _: WHOLE, out),
        out_shape=out,
        scratch_shapes=[pltpu.VMEM(s.shape, s.dtype) for s in scratch],
        compiler_params=PARAMS,
        cost_estimate=cost(weight),
    )(*scalars, *operands, *later)


def prepare(place, coupling_x, coupling_y, planes, z_table, y_table):
    return pl.pallas_call(
        spectrum_kernel,
        in_specs=[SMEM] * 3 + [WHOLE] * 3,
        out_specs=(SMEM, SMEM, WHOLE, WHOLE),
        out_shape=(array(2 * RIM, RIM), array(RIM, RIM), array(2, RIM, RIM, N), PART),
        compiler_params=PARAMS,
        cost_estimate=COST,
    )(place, coupling_x, coupling_y, planes, z_table, y_table)


def cut_faces(place, field):
    out = (SIDE, PART, FACE, PART)
    return pl.pallas_call(
        cut_kernel,
        in_specs=[SMEM, pl.BlockSpec(memory_space=pltpu.HBM)],
        out_specs=(WHOLE,) * 4,
        out_shape=out,
        scratch_shapes=[pltpu.SemaphoreType.DMA((4,))],
        compiler_params=PARAMS,
        cost_estimate=COST,
    )(place, field)


def body(field, source, wave, coupling_x, coupling_y):
    n_gx = lax.axis_size("gx")
    n_gy = lax.axis_size("gy")
    gx = lax.axis_index("gx")
    gy = lax.axis_index("gy")
    odd = gx % 2
    near_pairs = [(i, i ^ 1) for i in range(n_gx)]
    far_pairs = [(i, ((i + 1) ^ 1) - 1) for i in range(1, n_gx - 1)]
    side_pairs = [(i, i ^ 1) for i in range(n_gy)]

    zf, zi, yf, yi = (jnp.asarray(t) for t in dft_tables())
    green = jnp.asarray(green_table())
    lines = jnp.asarray(green_lines())

    weights = jnp.stack([odd, 1 - odd]).astype(F32)
    span = CX - RIM
    place = jnp.stack([odd * span, (1 - odd) * span, (1 - gy) * (N - RIM), 1 - gy]).astype(jnp.int32)
    rims = side_tables(dft_tables()[2])

    side_out, first_out, near_out, second_raw = cut_faces(place, field)
    mix_x, mix_far, mix_y, second_out = prepare(place, coupling_x, coupling_y, second_raw, zf, yf)
    for step in range(2):
        side_in = lax.ppermute(side_out, "gy", side_pairs)
        first_in = lax.ppermute(first_out, "gx", far_pairs)
        near_in = lax.ppermute(near_out, "gx", near_pairs)
        second_in = lax.ppermute(second_out, "gx", far_pairs)
        rows = array(CX * RIM, 2 * N)

        def far_part(after):
            return call(
                first_kernel, (mix_far,), (first_in, zf, yf), FACE, after=after,
                weight=10 if step == 0 else 60,
            )

        first = far_part(place) if step == 1 else None
        hat = call(
            local_kernel, (weights, mix_x), (mix_y, field, source, wave, near_in, zf, yf), VOLUME,
            after=place if first is None else first, weight=5,
        )
        part = call(
            side_kernel, (place,), (mix_y, side_in, hat, zf, rims, green), VOLUME, (rows, rows), weight=30
        )
        if first is None:
            first = far_part(part)
        if step == 0:
            whole, first_out = call(
                early_kernel, (place, mix_far),
                (second_in, first, part, lines, field, wave, yi, zi), (FACE, PART), (PART,),
            )
            field, side_out, near_out, second_out = call(
                middle_kernel, (place,), (whole, part, green, field, wave, yi, zi, zf, yf),
                (VOLUME, SIDE, FACE, PART), (VOLUME,),
            )
        else:
            field = pl.pallas_call(
                last_kernel,
                in_specs=[SMEM] * 2 + [WHOLE] * 8,
                out_specs=pl.BlockSpec(memory_space=pltpu.HBM),
                out_shape=VOLUME,
                scratch_shapes=[
                    pltpu.VMEM(VOLUME.shape, F32),
                    pltpu.VMEM(VOLUME.shape, F32),
                    pltpu.SemaphoreType.DMA((3,)),
                ],
                compiler_params=PARAMS,
                cost_estimate=COST,
            )(place, mix_far, second_in, first, part, green, field, wave, yi, zi)
    return field


def solution(mesh):
    placed = (P(None, "gx", "gy", None), P(None, "gx", "gy", None), P("gx", "gy", None), P(), P())
    return jax.shard_map(
        body, mesh=mesh, in_specs=placed, out_specs=P(None, "gx", "gy", None), check_vma=False
    )
```

time: 110 us -> 93.6 us (0.85)
  waiting for transfers between devices: 22.6 us -> 8.1 us
  Pallas kernels: 66.8 us -> 59.8 us
  starting transfers between devices: 12.5 us -> 18.6 us
    ppermute x2, waiting for transfers between devices: 16.7 us -> 0.01 us  [body(): side_in = lax.ppermute(side_out, 'gy', side_pairs)]
    pallas_call x8 -> x11, Pallas kernels: 66.8 us -> 59.8 us  [the longest x8 46.1 us: call(): pl.pallas_call(kernel, in_specs=[SMEM] * len(scalars) + [WHOLE] * len(ope...]
    ppermute x2 -> x4, starting transfers between devices: 7.19 us -> 11.9 us  [the longest x2 7.07 us: body(): first_in = lax.ppermute(first_out, 'gx', far_pairs)]
    dynamic_slice x4 -> x0, local copies, waits for them, and re-layouts: 4.48 us -> none  [the longest x2 3.47 us: body(): lax.dynamic_slice_in_dim(field, (1 - odd) * (CX - RIM), RIM, axis=1)]
    unnamed x18 -> x28, local copies, waits for them, and re-layouts: 2.22 us -> 6.31 us
    ppermute x2 -> x4, waiting for transfers between devices: 5.89 us -> 8.09 us  [the longest x2 8.08 us: body(): first_in = lax.ppermute(first_out, 'gx', far_pairs)]
    ppermute x2, starting transfers between devices: 3.87 us -> 4.97 us  [body(): side_in = lax.ppermute(side_out, 'gy', side_pairs)]
  transfers between devices with their start and end apart: 6 -> 8, of which waited for: 2 -> 2; matrix products, arithmetic and copies ran while one was open for 2% -> 0% of each run, Pallas kernels for 31% -> 49%
where the time goes in v1:
time: 93.6 us; the launch traced here: 93.3 us
  Pallas kernels  59.8 us (64%)
  starting transfers between devices  18.6 us (20%)
  waiting for transfers between devices  8.1 us (9%)
  local copies, waits for them, and re-layouts  6.31 us (7%)
    pallas_call x8, Pallas kernels, call(): pl.pallas_call(kernel, in_specs=[SMEM] * len(scalars) + [WHOLE] * len(ope...  46.1 us
    pallas_call x1, Pallas kernels, body(): pl.pallas_call(last_kernel, in_specs=[SMEM] * 2 + [WHOLE] * 8, out_specs=...  10.5 us
    ppermute x2, waiting for transfers between devices, body(): first_in = lax.ppermute(first_out, 'gx', far_pairs)  8.08 us
    ppermute x2, starting transfers between devices, body(): first_in = lax.ppermute(first_out, 'gx', far_pairs)  7.07 us
    unnamed x28, local copies, waits for them, and re-layouts  6.31 us
    ppermute x2, starting transfers between devices, body(): side_in = lax.ppermute(side_out, 'gy', side_pairs)  4.97 us
    ppermute x2, starting transfers between devices, body(): second_in = lax.ppermute(second_out, 'gx', far_pairs)  4.8 us
    pallas_call x1, Pallas kernels, prepare(): pl.pallas_call(spectrum_kernel, in_specs=[SMEM] * 3 + [WHOLE] * 3, out_sp...  2.39 us
  transfers between devices with their start and end apart: 8, of which 2 were waited for; matrix products, arithmetic and copies ran while one was open for 0% of the time, Pallas kernels for 49%

profile of v1, /device:TPU:1, one launch (start us, length us, event | category | flops | bytes accessed | tf_op | source)
XLA Modules:
  0.0 93.3 jit_solution(13012167613430869384)
XLA Ops:
  0.0 0.1 pad_add_fusion.place_ref.after_ref
  0.1 2.2 %copy-done = f32[2,32,128,128]{3,2,1,0:T(8,128)S(1)} copy-done((f32[2,32,128,128]{3,2,1,0:T(8,128)S(1)}, f32[2,32,128,128]{3,2,1,0:T(8,128)}, u32[]{:S(2)}) %copy-start) | copy-done | bytes 4194328
  2.3 0.8 shard_map.118
  3.0 1.5 %collective-permute-start.3 = (f32[2,8,128,128]{3,2,1,0:T(8,128)S(1)}, f32[2,8,128,128]{3,2,1,0:T(8,128)S(1)}, u32[]{:S(2)}, u32[]{:S(2)}) collective-permute-start(f32[2,8,128,128]{3,2,1,0:T(8,128)S(1)} %get-tuple-element.26), channel_id=1, source_target_pairs={{0,2},{2,0},{4,6},{6,4},{8,10},{10,8},{12,14},{14,12},{16,18},{18,... | collective-permute-start | bytes 3145736 | tf_op jit(solution)/shard_map/ppermute | solution.py:533
  4.5 3.7 %collective-permute-start.2 = (f32[2,32,8,128]{3,2,1,0:T(8,128)S(1)}, f32[2,32,8,128]{3,2,1,0:T(8,128)S(1)}, u32[]{:S(2)}, u32[]{:S(2)}) collective-permute-start(f32[2,32,8,128]{3,2,1,0:T(8,128)S(1)} %get-tuple-element.24), channel_id=1, source_target_pairs={{0,1},{1,0},{2,3},{3,2},{4,5},{5,4},{6,7},{7,6},{8,9},{9,8},{10,11... | collective-permute-start | bytes 786440 | tf_op jit(solution)/shard_map/ppermute | solution.py:531
  8.3 0.9 %copy-done.4 = bf16[2,256,256]{2,1,0:T(8,128)(2,1)S(1)} copy-done((bf16[2,256,256]{2,1,0:T(8,128)(2,1)S(1)}, bf16[2,256,256]{2,1,0:T(8,128)(2,1)}, u32[]{:S(2)}) %copy-start.4) | copy-done | bytes 262168
  9.2 0.9 %copy-done.6 = bf16[2,256,256]{2,1,0:T(8,128)(2,1)S(1)} copy-done((bf16[2,256,256]{2,1,0:T(8,128)(2,1)S(1)}, bf16[2,256,256]{2,1,0:T(8,128)(2,1)}, u32[]{:S(2)}) %copy-start.6) | copy-done | bytes 262168
  10.2 2.4 %shard_map.119 = (f32[16,8]{1,0:T(8,128)S(1)}, f32[8,8]{1,0:T(8,128)S(1)}, f32[2,8,8,128]{3,2,1,0:T(8,128)S(1)}, f32[2,4,128,128]{3,2,1,0:T(8,128)S(1)}) custom-call(s32[4]{0:T(128)S(1)} %pad_add_fusion.place_ref.after_ref, f32[8,8]{1,0:T(8,128)S(1)} %copy-done.11, f32[8,8]{1,0:T(8,128)S(1)} %copy-done.12, ...), custom_call_target="tpu_custom_call" | custom-call | flops 1000000000 | bytes 1000000 | tf_op jit(solution)/shard_map/pallas_call | solution.py:486
  12.6 2.9 %collective-permute-start = (f32[2,4,128,128]{3,2,1,0:T(8,128)S(1)}, f32[2,4,128,128]{3,2,1,0:T(8,128)S(1)}, u32[]{:S(2)}, u32[]{:S(2)}) collective-permute-start(f32[2,4,128,128]{3,2,1,0:T(8,128)S(1)} %get-tuple-element.21), channel_id=1, source_target_pairs={{2,4},{4,2},{6,8},{8,6},{10,12},{12,10},{14,16},{16,14},{18,20},{2... | collective-permute-start | bytes 1572872 | tf_op jit(solution)/shard_map/ppermute | solution.py:534
  15.4 2.7 %collective-permute-start.1 = (f32[2,4,128,128]{3,2,1,0:T(8,128)S(1)}, f32[2,4,128,128]{3,2,1,0:T(8,128)S(1)}, u32[]{:S(2)}, u32[]{:S(2)}) collective-permute-start(f32[2,4,128,128]{3,2,1,0:T(8,128)S(1)} %get-tuple-element.22), channel_id=1, source_target_pairs={{2,4},{4,2},{6,8},{8,6},{10,12},{12,10},{14,16},{16,14},{18,20},{2... | collective-permute-start | bytes 1572872 | tf_op jit(solution)/shard_map/ppermute | solution.py:532
  18.1 0.1 add_convert_fusion.side_ref
  18.2 0.0 copy-start.9
  18.2 2.2 %copy-done.9 = f32[2,32,128,128]{3,2,1,0:T(8,128)S(1)} copy-done((f32[2,32,128,128]{3,2,1,0:T(8,128)S(1)}, f32[2,32,128,128]{3,2,1,0:T(8,128)}, u32[]{:S(2)}) %copy-start.9) | copy-done | bytes 4194328
  20.4 7.7 %shard_map.120.hat_ref = f32[2,32,128,128]{3,2,1,0:T(8,128)S(1)} custom-call(f32[2]{0:T(128)S(1)} %add_convert_fusion.side_ref, f32[16,8]{1,0:T(8,128)S(1)} %get-tuple-element.25.mix_x_ref, f32[2,8,8,128]{3,2,1,0:T(8,128)S(1)} %get-tuple-element.23.mix_y_ref, f32[2,32,128,128]{3,2,1,0:T(8,128)S(1)} %copy-done.1, f32[2,32,128,128]{3,2,1,0:T(8,128)S(1)} %copy-done.9, ...), custom_call_target="tpu_custom_call" | custom-call | flops 5000000000 | bytes 5000000 | tf_op jit(solution)/shard_map/pallas_call | solution.py:473
  28.1 0.0 copy-start.7
  28.1 0.0 collective-permute-done.2.face_ref
  28.1 6.7 %shard_map.121.after_ref.part_ref = f32[2,32,128,128]{3,2,1,0:T(8,128)S(1)} custom-call(s32[4]{0:T(128)S(1)} %pad_add_fusion.place_ref.after_ref, f32[2,8,8,128]{3,2,1,0:T(8,128)S(1)} %get-tuple-element.23.mix_y_ref, f32[2,32,8,128]{3,2,1,0:T(8,128)S(1)} %collective-permute-done.2.face_ref, f32[2,32,128,128]{3,2,1,0:T(8,128)S(1)} %shard_map.120.hat_ref, ...), custom_call_target="tpu_custom_call" | custom-call | flops 30000001024 | bytes 30000000 | tf_op jit(solution)/shard_map/pallas_call | solution.py:473
  34.9 3.5 %collective-permute-done.1.face_ref = f32[2,4,128,128]{3,2,1,0:T(8,128)S(1)} collective-permute-done((f32[2,4,128,128]{3,2,1,0:T(8,128)S(1)}, f32[2,4,128,128]{3,2,1,0:T(8,128)S(1)}, u32[]{:S(2)}, u32[]{:S(2)}) %collective-permute-start.1) | collective-permute-done | bytes 524320 | tf_op jit(solution)/shard_map/ppermute | solution.py:532
  38.4 2.7 %shard_map.122.first_ref = f32[2,8,128,128]{3,2,1,0:T(8,128)S(1)} custom-call(f32[8,8]{1,0:T(8,128)S(1)} %get-tuple-element.20.mix_ref, f32[2,4,128,128]{3,2,1,0:T(8,128)S(1)} %collective-permute-done.1.face_ref, bf16[2,256,256]{2,1,0:T(8,128)(2,1)S(1)} %copy-done.5, bf16[2,256,256]{2,1,0:T(8,128)(2,1)S(1)} %copy-done.7, ...), custom_call_target="tpu_custom_call" | custom-call | flops 10000000000 | bytes 10000000 | tf_op jit(solution)/shard_map/pallas_call | solution.py:473
  41.1 0.0 collective-permute-done.second_ref
  41.1 2.7 %shard_map.123 = (f32[2,8,128,128]{3,2,1,0:T(8,128)S(1)}, f32[2,4,128,128]{3,2,1,0:T(8,128)S(1)}) custom-call(s32[4]{0:T(128)S(1)} %pad_add_fusion.place_ref.after_ref, f32[8,8]{1,0:T(8,128)S(1)} %get-tuple-element.20.mix_ref, f32[2,4,128,128]{3,2,1,0:T(8,128)S(1)} %collective-permute-done.second_ref, f32[2,8,128,128]{3,2,1,0:T(8,128)S(1)} %shard_map.122.first_ref, ...), custom_call_target="tpu_custom_call" | custom-call | flops 1000000000 | bytes 1000000 | tf_op jit(solution)/shard_map/pallas_call | solution.py:473
  43.8 4.4 %collective-permute-start.5 = (f32[2,4,128,128]{3,2,1,0:T(8,128)S(1)}, f32[2,4,128,128]{3,2,1,0:T(8,128)S(1)}, u32[]{:S(2)}, u32[]{:S(2)}) collective-permute-start(f32[2,4,128,128]{3,2,1,0:T(8,128)S(1)} %get-tuple-element.29), channel_id=1, source_target_pairs={{2,4},{4,2},{6,8},{8,6},{10,12},{12,10},{14,16},{16,14},{18,20},{2... | collective-permute-start | bytes 1572872 | tf_op jit(solution)/shard_map/ppermute | solution.py:532
  48.2 9.2 %shard_map.124 = (f32[2,32,128,128]{3,2,1,0:T(8,128)S(1)}, f32[2,32,8,128]{3,2,1,0:T(8,128)S(1)}, f32[2,8,128,128]{3,2,1,0:T(8,128)S(1)}, f32[2,4,128,128]{3,2,1,0:T(8,128)S(1)}) custom-call(s32[4]{0:T(128)S(1)} %pad_add_fusion.place_ref.after_ref, f32[2,8,128,128]{3,2,1,0:T(8,128)S(1)} %get-tuple-element.27.hat_ref, ...), custom_call_target="tpu_custom_call" | custom-call | flops 1000000000 | bytes 1000000 | tf_op jit(solution)/shard_map/pallas_call | solution.py:473
  57.5 1.3 %collective-permute-start.6 = (f32[2,32,8,128]{3,2,1,0:T(8,128)S(1)}, f32[2,32,8,128]{3,2,1,0:T(8,128)S(1)}, u32[]{:S(2)}, u32[]{:S(2)}) collective-permute-start(f32[2,32,8,128]{3,2,1,0:T(8,128)S(1)} %get-tuple-element.30), channel_id=1, source_target_pairs={{0,1},{1,0},{2,3},{3,2},{4,5},{5,4},{6,7},{7,6},{8,9},{9,8},{10,11... | collective-permute-start | bytes 786440 | tf_op jit(solution)/shard_map/ppermute | solution.py:531
  58.7 1.9 %collective-permute-start.4 = (f32[2,4,128,128]{3,2,1,0:T(8,128)S(1)}, f32[2,4,128,128]{3,2,1,0:T(8,128)S(1)}, u32[]{:S(2)}, u32[]{:S(2)}) collective-permute-start(f32[2,4,128,128]{3,2,1,0:T(8,128)S(1)} %get-tuple-element.28), channel_id=1, source_target_pairs={{2,4},{4,2},{6,8},{8,6},{10,12},{12,10},{14,16},{16,14},{18,20},{2... | collective-permute-start | bytes 1572872 | tf_op jit(solution)/shard_map/ppermute | solution.py:534
  60.7 0.0 copy-start.10
  60.7 0.3 collective-permute-start.7
  60.9 4.6 %collective-permute-done.5.face_ref = f32[2,4,128,128]{3,2,1,0:T(8,128)S(1)} collective-permute-done((f32[2,4,128,128]{3,2,1,0:T(8,128)S(1)}, f32[2,4,128,128]{3,2,1,0:T(8,128)S(1)}, u32[]{:S(2)}, u32[]{:S(2)}) %collective-permute-start.5) | collective-permute-done | bytes 524320 | tf_op jit(solution)/shard_map/ppermute | solution.py:532
  65.5 2.7 %shard_map.125.after_ref.first_ref = f32[2,8,128,128]{3,2,1,0:T(8,128)S(1)} custom-call(f32[8,8]{1,0:T(8,128)S(1)} %get-tuple-element.20.mix_ref, f32[2,4,128,128]{3,2,1,0:T(8,128)S(1)} %collective-permute-done.5.face_ref, bf16[2,256,256]{2,1,0:T(8,128)(2,1)S(1)} %copy-done.5, bf16[2,256,256]{2,1,0:T(8,128)(2,1)S(1)} %copy-done.7, ...), custom_call_target="tpu_custom_call" | custom-call | flops 60000002048 | bytes 60000000 | tf_op jit(solution)/shard_map/pallas_call | solution.py:473
  68.2 7.6 %shard_map.126.hat_ref = f32[2,32,128,128]{3,2,1,0:T(8,128)S(1)} custom-call(f32[2]{0:T(128)S(1)} %add_convert_fusion.side_ref, f32[16,8]{1,0:T(8,128)S(1)} %get-tuple-element.25.mix_x_ref, f32[2,8,8,128]{3,2,1,0:T(8,128)S(1)} %get-tuple-element.23.mix_y_ref, f32[2,32,128,128]{3,2,1,0:T(8,128)S(1)} %get-tuple-element.31.field_ref, ...), custom_call_target="tpu_custom_call" | custom-call | flops 5000000000 | bytes 5000000 | tf_op jit(solution)/shard_map/pallas_call | solution.py:473
  75.8 6.7 %shard_map.127.part_ref = f32[2,32,128,128]{3,2,1,0:T(8,128)S(1)} custom-call(s32[4]{0:T(128)S(1)} %pad_add_fusion.place_ref.after_ref, f32[2,8,8,128]{3,2,1,0:T(8,128)S(1)} %get-tuple-element.23.mix_y_ref, f32[2,32,8,128]{3,2,1,0:T(8,128)S(1)} %collective-permute-done.6.face_ref, f32[2,32,128,128]{3,2,1,0:T(8,128)S(1)} %shard_map.126.hat_ref, ...), custom_call_target="tpu_custom_call" | custom-call | flops 30000001024 | bytes 30000000 | tf_op jit(solution)/shard_map/pallas_call | solution.py:473
  82.6 10.5 %shard_map.128 = f32[2,32,128,128]{3,2,1,0:T(8,128)} custom-call(s32[4]{0:T(128)S(1)} %pad_add_fusion.place_ref.after_ref, f32[8,8]{1,0:T(8,128)S(1)} %get-tuple-element.20.mix_ref, f32[2,4,128,128]{3,2,1,0:T(8,128)S(1)} %collective-permute-done.4.second_ref, f32[2,8,128,128]{3,2,1,0:T(8,128)S(1)} %shard_map.125.after_ref.first_ref, ...), custom_call_target="tpu_custom_call" | custom-call | flops 1000000000 | bytes 1000000 | tf_op jit(solution)/shard_map/pallas_call | solution.py:563
  (25 shorter events, 0.0 us)
Async XLA Ops:
  0.0 8.2 %copy-start.12 = (f32[8,8]{1,0:T(8,128)S(1)}, f32[8,8]{1,0:T(8,128)}, u32[]{:S(2)}) copy-start(f32[8,8]{1,0:T(8,128)} %y_coupling_ref.1) | copy-start | bytes 772
  0.0 8.2 %copy-start.11 = (f32[8,8]{1,0:T(8,128)S(1)}, f32[8,8]{1,0:T(8,128)}, u32[]{:S(2)}) copy-start(f32[8,8]{1,0:T(8,128)} %x_ref.1) | copy-start | bytes 772
  0.1 2.2 %copy-start = (f32[2,32,128,128]{3,2,1,0:T(8,128)S(1)}, f32[2,32,128,128]{3,2,1,0:T(8,128)}, u32[]{:S(2)}) copy-start(f32[2,32,128,128]{3,2,1,0:T(8,128)} %field_ref.7) | copy-start | bytes 12582916
  2.3 15.9 %copy-start.1 = (f32[2,32,128,128]{3,2,1,0:T(8,128)S(1)}, f32[2,32,128,128]{3,2,1,0:T(8,128)}, u32[]{:S(2)}) copy-start(f32[2,32,128,128]{3,2,1,0:T(8,128)} %field_ref.7) | copy-start | bytes 12582916
  2.3 15.9 %copy-start.2 = (f32[32,128,128]{2,1,0:T(8,128)S(1)}, f32[32,128,128]{2,1,0:T(8,128)}, u32[]{:S(2)}) copy-start(f32[32,128,128]{2,1,0:T(8,128)} %wave_ref.9) | copy-start | bytes 6291460
  3.0 15.2 %collective-permute-start.3 = (f32[2,8,128,128]{3,2,1,0:T(8,128)S(1)}, f32[2,8,128,128]{3,2,1,0:T(8,128)S(1)}, u32[]{:S(2)}, u32[]{:S(2)}) collective-permute-start(f32[2,8,128,128]{3,2,1,0:T(8,128)S(1)} %get-tuple-element.26), channel_id=1, source_target_pairs={{0,2},{2,0},{4,6},{6,4},{8,10},{10,8},{12,14},{14,12},{16,18},{18,... | collective-permute-start | bytes 3145736 | tf_op jit(solution)/shard_map/ppermute | solution.py:533
  4.5 23.6 %collective-permute-start.2 = (f32[2,32,8,128]{3,2,1,0:T(8,128)S(1)}, f32[2,32,8,128]{3,2,1,0:T(8,128)S(1)}, u32[]{:S(2)}, u32[]{:S(2)}) collective-permute-start(f32[2,32,8,128]{3,2,1,0:T(8,128)S(1)} %get-tuple-element.24), channel_id=1, source_target_pairs={{0,1},{1,0},{2,3},{3,2},{4,5},{5,4},{6,7},{7,6},{8,9},{9,8},{10,11... | collective-permute-start | bytes 786440 | tf_op jit(solution)/shard_map/ppermute | solution.py:531
  8.2 1.0 %copy-start.4 = (bf16[2,256,256]{2,1,0:T(8,128)(2,1)S(1)}, bf16[2,256,256]{2,1,0:T(8,128)(2,1)}, u32[]{:S(2)}) copy-start(bf16[2,256,256]{2,1,0:T(8,128)(2,1)} %constant.36.clone.z_ref.y_ref.yi_ref) | copy-start | bytes 786436
  9.2 0.9 %copy-start.6 = (bf16[2,256,256]{2,1,0:T(8,128)(2,1)S(1)}, bf16[2,256,256]{2,1,0:T(8,128)(2,1)}, u32[]{:S(2)}) copy-start(bf16[2,256,256]{2,1,0:T(8,128)(2,1)} %constant.37.clone.y_ref.z_ref.zi_ref) | copy-start | bytes 786436
  12.6 28.5 %collective-permute-start = (f32[2,4,128,128]{3,2,1,0:T(8,128)S(1)}, f32[2,4,128,128]{3,2,1,0:T(8,128)S(1)}, u32[]{:S(2)}, u32[]{:S(2)}) collective-permute-start(f32[2,4,128,128]{3,2,1,0:T(8,128)S(1)} %get-tuple-element.21), channel_id=1, source_target_pairs={{2,4},{4,2},{6,8},{8,6},{10,12},{12,10},{14,16},{16,14},{18,20},{2... | collective-permute-start | bytes 1572872 | tf_op jit(solution)/shard_map/ppermute | solution.py:534
  15.4 23.0 %collective-permute-start.1 = (f32[2,4,128,128]{3,2,1,0:T(8,128)S(1)}, f32[2,4,128,128]{3,2,1,0:T(8,128)S(1)}, u32[]{:S(2)}, u32[]{:S(2)}) collective-permute-start(f32[2,4,128,128]{3,2,1,0:T(8,128)S(1)} %get-tuple-element.22), channel_id=1, source_target_pairs={{2,4},{4,2},{6,8},{8,6},{10,12},{12,10},{14,16},{16,14},{18,20},{2... | collective-permute-start | bytes 1572872 | tf_op jit(solution)/shard_map/ppermute | solution.py:532
  18.2 2.2 %copy-start.9 = (f32[2,32,128,128]{3,2,1,0:T(8,128)S(1)}, f32[2,32,128,128]{3,2,1,0:T(8,128)}, u32[]{:S(2)}) copy-start(f32[2,32,128,128]{3,2,1,0:T(8,128)} %source_ref.3) | copy-start | bytes 12582916
  20.4 7.7 %copy-start.3 = (f32[17,2,128,128]{3,2,1,0:T(8,128)S(1)}, f32[17,2,128,128]{3,2,1,0:T(8,128)}, u32[]{:S(2)}) copy-start(f32[17,2,128,128]{3,2,1,0:T(8,128)} %constant.38.clone.green_ref) | copy-start | bytes 6684676
  20.4 7.7 %copy-start.5 = (bf16[2,256,256]{2,1,0:T(8,128)(2,1)S(1)}, bf16[2,256,256]{2,1,0:T(8,128)(2,1)}, u32[]{:S(2)}) copy-start(bf16[2,256,256]{2,1,0:T(8,128)(2,1)} %constant.36.clone.z_ref.y_ref.yi_ref) | copy-start | bytes 786436
  20.4 7.7 %copy-start.13 = (bf16[2,2,256,16]{3,2,1,0:T(8,128)(2,1)S(1)}, bf16[2,2,256,16]{3,2,1,0:T(8,128)(2,1)}, u32[]{:S(2)}) copy-start(bf16[2,2,256,16]{3,2,1,0:T(8,128)(2,1)} %constant.40.clone.table_ref) | copy-start | bytes 98308
  28.1 10.3 %copy-start.7 = (bf16[2,256,256]{2,1,0:T(8,128)(2,1)S(1)}, bf16[2,256,256]{2,1,0:T(8,128)(2,1)}, u32[]{:S(2)}) copy-start(bf16[2,256,256]{2,1,0:T(8,128)(2,1)} %constant.37.clone.y_ref.z_ref.zi_ref) | copy-start | bytes 786436
  38.4 2.7 %copy-start.8 = (f32[8,2,128,128]{3,2,1,0:T(8,128)S(1)}, f32[8,2,128,128]{3,2,1,0:T(8,128)}, u32[]{:S(2)}) copy-start(f32[8,2,128,128]{3,2,1,0:T(8,128)} %constant.39.clone.line_ref) | copy-start | bytes 3145732
  43.8 21.7 %collective-permute-start.5 = (f32[2,4,128,128]{3,2,1,0:T(8,128)S(1)}, f32[2,4,128,128]{3,2,1,0:T(8,128)S(1)}, u32[]{:S(2)}, u32[]{:S(2)}) collective-permute-start(f32[2,4,128,128]{3,2,1,0:T(8,128)S(1)} %get-tuple-element.29), channel_id=1, source_target_pairs={{2,4},{4,2},{6,8},{8,6},{10,12},{12,10},{14,16},{16,14},{18,20},{2... | collective-permute-start | bytes 1572872 | tf_op jit(solution)/shard_map/ppermute | solution.py:532
  57.5 18.4 %collective-permute-start.6 = (f32[2,32,8,128]{3,2,1,0:T(8,128)S(1)}, f32[2,32,8,128]{3,2,1,0:T(8,128)S(1)}, u32[]{:S(2)}, u32[]{:S(2)}) collective-permute-start(f32[2,32,8,128]{3,2,1,0:T(8,128)S(1)} %get-tuple-element.30), channel_id=1, source_target_pairs={{0,1},{1,0},{2,3},{3,2},{4,5},{5,4},{6,7},{7,6},{8,9},{9,8},{10,11... | collective-permute-start | bytes 786440 | tf_op jit(solution)/shard_map/ppermute | solution.py:531
  58.7 23.9 %collective-permute-start.4 = (f32[2,4,128,128]{3,2,1,0:T(8,128)S(1)}, f32[2,4,128,128]{3,2,1,0:T(8,128)S(1)}, u32[]{:S(2)}, u32[]{:S(2)}) collective-permute-start(f32[2,4,128,128]{3,2,1,0:T(8,128)S(1)} %get-tuple-element.28), channel_id=1, source_target_pairs={{2,4},{4,2},{6,8},{8,6},{10,12},{12,10},{14,16},{16,14},{18,20},{2... | collective-permute-start | bytes 1572872 | tf_op jit(solution)/shard_map/ppermute | solution.py:534
  60.7 7.5 %copy-start.10 = (f32[2,32,128,128]{3,2,1,0:T(8,128)S(1)}, f32[2,32,128,128]{3,2,1,0:T(8,128)}, u32[]{:S(2)}) copy-start(f32[2,32,128,128]{3,2,1,0:T(8,128)} %source_ref.3) | copy-start | bytes 12582916
  60.7 7.5 %collective-permute-start.7 = (f32[2,8,128,128]{3,2,1,0:T(8,128)S(1)}, f32[2,8,128,128]{3,2,1,0:T(8,128)S(1)}, u32[]{:S(2)}, u32[]{:S(2)}) collective-permute-start(f32[2,8,128,128]{3,2,1,0:T(8,128)S(1)} %get-tuple-element.32), channel_id=1, source_target_pairs={{0,2},{2,0},{4,6},{6,4},{8,10},{10,8},{12,14},{14,12},{16,18},{18,... | collective-permute-start | bytes 3145736 | tf_op jit(solution)/shard_map/ppermute | solution.py:533

commit v2 on v1

--- a/solution.py
+++ b/solution.py
@@ -3,7 +3,6 @@
 
 import jax
 import jax.numpy as jnp
-import ml_dtypes
 import numpy as np
 from jax import lax
 from jax.experimental import pallas as pl
@@ -11,7 +10,9 @@
 from jax.sharding import PartitionSpec as P
 
 RIM = 8
-HALF = 4
+LEAD = 3
+REST = RIM - LEAD
+RING = 4
 K0SQ = 2.4674
 EPS = 2.5
 CX = 32
@@ -21,34 +22,13 @@
 VMEM_LIMIT = 24 * 1024 * 1024
 
 
-def two_halves(table):
-    high = table.astype(ml_dtypes.bfloat16)
-    low = (table - high.astype(np.float64)).astype(ml_dtypes.bfloat16)
-    return np.stack([high, low])
-
-
 def dft_tables():
     index = np.arange(N)
     angle = 2.0 * np.pi / N * (index[:, None] * index[None, :] % N)
     cosine, sine = np.cos(angle), np.sin(angle)
-    z_forward = np.block([[cosine, -sine], [sine, cosine]])
-    z_inverse = np.block([[cosine, sine], [-sine, cosine]])
-    return (
-        two_halves(z_forward),
-        two_halves(z_inverse),
-        two_halves(z_forward.T),
-        two_halves(z_inverse.T),
-    )
-
-
-def side_tables(table):
-    table = table.reshape(2, 2 * N, 2, N)
-    return np.stack(
-        [
-            table[:, :, :, rows].reshape(2, 2 * N, 2 * RIM)
-            for rows in (slice(0, RIM), slice(N - RIM, N))
-        ]
-    )
+    forward = np.block([[cosine, -sine], [sine, cosine]])
+    inverse = np.block([[cosine, sine], [-sine, cosine]])
+    return forward, inverse
 
 
 def angular_sq(length):
@@ -192,14 +172,12 @@
     return total
 
 
-def cut_kernel(place_ref, field_ref, side_ref, first_ref, near_ref, second_ref, sems):
-    far, near, rows = place_ref[0], place_ref[1], place_ref[2]
-    rows = pl.multiple_of(rows, RIM)
+def cut_kernel(place_ref, field_ref, side_ref, first_ref, near_ref, sems):
+    far, near, rows = place_ref[0], place_ref[1], pl.multiple_of(place_ref[2], RIM)
     copies = [
         pltpu.make_async_copy(field_ref.at[:, :, pl.ds(rows, RIM), :], side_ref, sems.at[0]),
-        pltpu.make_async_copy(field_ref.at[:, pl.ds(far, HALF)], first_ref, sems.at[1]),
-        pltpu.make_async_copy(field_ref.at[:, pl.ds(far + HALF, HALF)], second_ref, sems.at[2]),
-        pltpu.make_async_copy(field_ref.at[:, pl.ds(near, RIM)], near_ref, sems.at[3]),
+        pltpu.make_async_copy(field_ref.at[:, pl.ds(far, LEAD)], first_ref, sems.at[1]),
+        pltpu.make_async_copy(field_ref.at[:, pl.ds(near, RIM)], near_ref, sems.at[2]),
     ]
     for copy in copies:
         copy.start()
@@ -217,34 +195,44 @@
 
 
 def spectrum_kernel(
-    place_ref, x_ref, y_coupling_ref, planes_ref, z_ref, y_ref, mix_x_ref, mix_far_ref, mix_y_ref, out_ref
+    place_ref, x_ref, y_coupling_ref, field_ref, forward_ref, inverse_ref, after_ref,
+    mix_x_ref, mix_far_ref, mix_y_ref, out_ref, z_ref, y_ref, planes_ref, sem,
 ):
-    odd = place_ref[0] > 0
+    far = place_ref[0]
+    copy = pltpu.make_async_copy(field_ref.at[:, pl.ds(far + LEAD, REST)], planes_ref, sem)
+    copy.start()
+    odd = far > 0
     for a in range(RIM):
         for b in range(RIM):
             low, high = x_ref[a, RIM - 1 - b], x_ref[RIM - 1 - a, b]
             mix_x_ref[a, b] = low
             mix_x_ref[RIM + a, b] = high
             mix_far_ref[a, b] = jnp.where(odd, high, low)
+    for table_ref, halves_ref in ((forward_ref, z_ref), (inverse_ref, y_ref)):
+        halves_ref[0], halves_ref[1] = halves(table_ref[...])
     for side in range(2):
         for b in range(RIM):
             mix_y_ref[side, b] = by_depth(y_coupling_ref, side, b)
-    planes = [(planes_ref[0, k], planes_ref[1, k]) for k in range(HALF)]
+    copy.wait()
+    planes = [(planes_ref[0, k], planes_ref[1, k]) for k in range(REST)]
     for k, (re, im) in enumerate(y_product(z_product(planes, z_ref), y_ref)):
         out_ref[0, k] = re
         out_ref[1, k] = im
 
 
 def local_kernel(
-    side_ref, mix_x_ref, mix_y_ref, field_ref, source_ref, wave_ref, near_ref, z_ref, y_ref, after_ref,
-    out_ref,
+    side_ref, place_ref, mix_x_ref, mix_y_ref, field_ref, source_ref, wave_ref, near_ref, z_ref,
+    after_ref, out_ref,
 ):
+    base = place_ref[0]
+
     @pl.loop(0, CX)
     def _(x):
         shifted = wave_ref[x] - K0SQ
         re, im = field_ref[0, x], field_ref[1, x]
-        out_ref[0, x] = shifted * re + EPS * im + source_ref[0, x]
-        out_ref[1, x] = shifted * im - EPS * re + source_ref[1, x]
+        to = lax.rem(x + CX - base, CX)
+        out_ref[0, to] = shifted * re + EPS * im + source_ref[0, x]
+        out_ref[1, to] = shifted * im - EPS * re + source_ref[1, x]
         for part in range(2):
             first = field_ref[part, x, 0:RIM, :]
             last = field_ref[part, x, N - RIM : N, :]
@@ -253,11 +241,12 @@
             for b in range(1, RIM):
                 add_low += mix_y_ref[0, b] * last[b : b + 1]
                 add_high += mix_y_ref[1, b] * first[b : b + 1]
-            out_ref[part, x, 0:RIM, :] += add_low
-            out_ref[part, x, N - RIM : N, :] += add_high
-
-    for side, base, other in ((0, 0, CX - RIM), (1, CX - RIM, 0)):
+            out_ref[part, to, 0:RIM, :] += add_low
+            out_ref[part, to, N - RIM : N, :] += add_high
+
+    for side, start, other in ((0, 0, CX - RIM), (1, CX - RIM, 0)):
         weight = side_ref[side]
+        to = lax.rem(start + CX - base, CX)
 
         @tiles(N, 16)
         def _(rows):
@@ -267,40 +256,46 @@
                     for r in range(RIM)
                 ]
                 for p in range(RIM):
-                    out_ref[part, base + p, rows, :] += mixed(mix_x_ref, side * RIM + p, 0, source)
+                    out_ref[part, to + p, rows, :] += mixed(mix_x_ref, side * RIM + p, 0, source)
 
     transform(z_product, z_ref, out_ref, CX, 16)
-    transform(y_product, y_ref, out_ref, CX, 16)
 
 
 def side_kernel(
-    place_ref, mix_y_ref, face_ref, hat_ref, z_ref, table_ref, green_ref, out_ref, rows_ref, wide_ref
+    side_ref, place_ref, mix_y_ref, face_ref, hat_ref, z_ref, y_ref, green_ref, out_ref, rows_ref, wide_ref
 ):
-    upper = place_ref[3]
-    mix_ref, table_ref = mix_y_ref.at[upper], table_ref.at[upper]
+    mix_ref = mix_y_ref.at[place_ref[3]]
 
     @pl.loop(0, CX)
     def _(x):
         for part in range(2):
-            tile = face_ref[part, x]
+            tile = face_ref[part, lax.rem(x + place_ref[0], CX)]
             total = mix_ref[0] * tile[0:1]
             for b in range(1, RIM):
                 total += mix_ref[b] * tile[b : b + 1]
             rows_ref[pl.ds(pl.multiple_of(x * RIM, RIM), RIM), part * N : (part + 1) * N] = -total
 
     wide_ref[...] = from_right(rows_ref[...], z_ref)
-
-    group = 8
+    low, high = side_ref[2], side_ref[3]
+    group = 16
+
+    def with_side(part, x, term):
+        value = hat_ref[part, x]
+        return jnp.concatenate(
+            [value[:RIM] + low * term, value[RIM : N - RIM], value[N - RIM :] + high * term], axis=0
+        )
 
     @pl.loop(0, CX // group)
     def _(i):
-        rows = wide_ref[pl.ds(pl.multiple_of(i * group * RIM, group * RIM), group * RIM), :]
-        parts = [rows[k * RIM : (k + 1) * RIM] for k in range(group)]
-        short = [(part[:, :N], part[:, N:]) for part in parts]
-        for k, (re, im) in enumerate(y_product(short, table_ref)):
+        terms = wide_ref[pl.ds(pl.multiple_of(i * group * RIM, group * RIM), group * RIM), :]
+        planes = []
+        for k in range(group):
+            term = terms[k * RIM : (k + 1) * RIM]
             x = i * group + k
-            out_ref[0, x] = hat_ref[0, x] + re
-            out_ref[1, x] = hat_ref[1, x] + im
+            planes.append((with_side(0, x, term[:, :N]), with_side(1, x, term[:, N:])))
+        for k, (re, im) in enumerate(y_product(planes, y_ref)):
+            out_ref[0, i * group + k] = re
+            out_ref[1, i * group + k] = im
 
     @tiles(N, 8)
     def _(rows):
@@ -314,7 +309,7 @@
     @tiles(N, 16)
     def _(rows):
         for part in range(2):
-            source = [face_ref[part, r, rows, :] for r in range(HALF)]
+            source = [face_ref[part, r, rows, :] for r in range(LEAD)]
             for p in range(RIM):
                 out_ref[part, p, rows, :] = -mixed(mix_ref, p, 0, source)
 
@@ -337,19 +332,19 @@
     @tiles(N, 8)
     def _(rows):
         for part in range(2):
-            source = [second_ref[part, r, rows, :] for r in range(HALF)]
+            source = [second_ref[part, r, rows, :] for r in range(REST)]
             for p in range(RIM):
                 hat_ref[part, p, rows, :] = first_ref[part, p, rows, :] - mixed(
-                    mix_ref, p, HALF, source
+                    mix_ref, p, LEAD, source
                 )
 
     @tiles(N, 8)
     def _(rows):
         given = [(hat_ref[0, p, rows, :], hat_ref[1, p, rows, :]) for p in range(RIM)]
         lines = [(line_ref[d, 0, rows, :], line_ref[d, 1, rows, :]) for d in range(RIM)]
-        for p in range(HALF):
-            re = part_ref[0, base + p, rows, :]
-            im = part_ref[1, base + p, rows, :]
+        for p in range(LEAD):
+            re = part_ref[0, p, rows, :]
+            im = part_ref[1, p, rows, :]
             for q, (t_re, t_im) in enumerate(given):
                 g_re, g_im = lines[abs(p - q)]
                 re += t_re * g_re - t_im * g_im
@@ -357,55 +352,57 @@
             work_ref[0, p, rows, :] = re
             work_ref[1, p, rows, :] = im
 
-    planes = [(work_ref[0, k], work_ref[1, k]) for k in range(HALF)]
+    planes = [(work_ref[0, k], work_ref[1, k]) for k in range(LEAD)]
     for k, back in enumerate(z_product(y_product(planes, y_ref), z_ref)):
         re, im = damped(field_ref[0, base + k], field_ref[1, base + k], back, wave_ref[base + k])
         out_ref[0, k] = re
         out_ref[1, k] = im
 
 
-def filter_far(base, given_of, part_ref, green_ref, work_ref):
-    @tiles(N, 8)
-    def _(rows):
-        spectrum = fft_of_first(given_of(rows), CX)
-        for k, (re, im) in enumerate(filtered(spectrum, green_ref, rows)):
-            x = lax.rem(base + k, CX)
-            work_ref[0, x, rows, :] = part_ref[0, x, rows, :] + re
-            work_ref[1, x, rows, :] = part_ref[1, x, rows, :] + im
-
-
-def step_back(work_ref, field_ref, wave_ref, y_ref, z_ref, out_ref):
-    group = 16
-    transform(y_product, y_ref, work_ref, CX, group)
-
-    @pl.loop(0, CX // group)
+def filter_far(given_of, part_ref, green_ref, z_ref, ring_refs, work_ref):
+    ring = len(ring_refs)
+
+    @pl.loop(0, N // (8 * ring))
     def _(i):
-        first = i * group
-        planes = [(work_ref[0, first + k], work_ref[1, first + k]) for k in range(group)]
-        for k, back in enumerate(z_product(planes, z_ref)):
-            x = first + k
-            re, im = damped(field_ref[0, x], field_ref[1, x], back, wave_ref[x])
-            out_ref[0, x] = re
-            out_ref[1, x] = im
+        for j, ring_ref in enumerate(ring_refs):
+            rows = pl.ds(pl.multiple_of(i * 8 * ring, 8 * ring) + 8 * j, 8)
+            spectrum = fft_of_first(given_of(rows), CX)
+            for x, (re, im) in enumerate(filtered(spectrum, green_ref, rows)):
+                ring_ref[0, x] = part_ref[0, x, rows, :] + re
+                ring_ref[1, x] = part_ref[1, x, rows, :] + im
+            planes = [(ring_ref[0, x], ring_ref[1, x]) for x in range(CX)]
+            for x, (re, im) in enumerate(z_product(planes, z_ref)):
+                work_ref[0, x, rows, :] = re
+                work_ref[1, x, rows, :] = im
+
+
+def step_back(base, first, group, work_ref, field_ref, wave_ref, y_ref, out_ref):
+    planes = [(work_ref[0, first + k], work_ref[1, first + k]) for k in range(group)]
+    for k, back in enumerate(y_product(planes, y_ref)):
+        x = lax.rem(first + k + base, CX)
+        re, im = damped(field_ref[0, x], field_ref[1, x], back, wave_ref[x])
+        out_ref[0, x] = re
+        out_ref[1, x] = im
 
 
 def middle_kernel(
     place_ref, hat_ref, part_ref, green_ref, field_ref, wave_ref, yi_ref, zi_ref, z_ref, y_ref,
-    out_ref, side_ref, near_ref, second_ref, work_ref,
+    out_ref, side_ref, near_ref, second_ref, work_ref, *ring_refs,
 ):
     base = place_ref[0]
 
     def given_of(rows):
         return [(hat_ref[0, p, rows, :], hat_ref[1, p, rows, :]) for p in range(RIM)]
 
-    filter_far(base, given_of, part_ref, green_ref, work_ref)
-    step_back(work_ref, field_ref, wave_ref, yi_ref, zi_ref, out_ref)
+    filter_far(given_of, part_ref, green_ref, zi_ref, ring_refs, work_ref)
+    for first in (0, 16):
+        step_back(base, first, 16, work_ref, field_ref, wave_ref, yi_ref, out_ref)
 
     cut = pl.ds(pl.multiple_of(place_ref[2], RIM), RIM)
     for part in range(2):
         side_ref[part] = out_ref[part, :, cut, :]
         near_ref[part] = out_ref[part, pl.ds(place_ref[1], RIM)]
-    planes = [(out_ref[0, base + k], out_ref[1, base + k]) for k in range(HALF, RIM)]
+    planes = [(out_ref[0, base + k], out_ref[1, base + k]) for k in range(LEAD, RIM)]
     for k, (re, im) in enumerate(y_product(z_product(planes, z_ref), y_ref)):
         second_ref[0, k] = re
         second_ref[1, k] = im
@@ -413,32 +410,25 @@
 
 def last_kernel(
     place_ref, mix_ref, second_ref, first_ref, part_ref, green_ref, field_ref, wave_ref, yi_ref, zi_ref,
-    out_ref, work_ref, done_ref, sems,
+    out_ref, work_ref, done_ref, sems, *ring_refs,
 ):
     def given_of(rows):
         sums = []
         for part in range(2):
-            source = [second_ref[part, r, rows, :] for r in range(HALF)]
+            source = [second_ref[part, r, rows, :] for r in range(REST)]
             sums.append(
-                [
-                    first_ref[part, p, rows, :] - mixed(mix_ref, p, HALF, source)
-                    for p in range(RIM)
-                ]
+                [first_ref[part, p, rows, :] - mixed(mix_ref, p, LEAD, source) for p in range(RIM)]
             )
         return list(zip(*sums))
 
-    filter_far(place_ref[0], given_of, part_ref, green_ref, work_ref)
-    transform(y_product, yi_ref, work_ref, CX, 16)
+    base = place_ref[0]
+    filter_far(given_of, part_ref, green_ref, zi_ref, ring_refs, work_ref)
     copies = []
-    for i, (first, group) in enumerate(((0, 16), (16, 8), (24, 8))):
-        planes = [(work_ref[0, first + k], work_ref[1, first + k]) for k in range(group)]
-        for k, back in enumerate(z_product(planes, zi_ref)):
-            x = first + k
-            re, im = damped(field_ref[0, x], field_ref[1, x], back, wave_ref[x])
-            done_ref[0, x] = re
-            done_ref[1, x] = im
-        span = pl.ds(first, group)
-        copies.append(pltpu.make_async_copy(done_ref.at[:, span], out_ref.at[:, span], sems.at[i]))
+    for first in range(0, CX, RIM):
+        step_back(base, first, RIM, work_ref, field_ref, wave_ref, yi_ref, done_ref)
+        span = pl.ds(lax.rem(base + first, CX), RIM)
+        sem = sems.at[first // RIM]
+        copies.append(pltpu.make_async_copy(done_ref.at[:, span], out_ref.at[:, span], sem))
         copies[-1].start()
     for copy in copies:
         copy.wait()
@@ -454,8 +444,10 @@
 
 VOLUME = array(2, CX, N, N)
 FACE = array(2, RIM, N, N)
-PART = array(2, HALF, N, N)
+PART = array(2, LEAD, N, N)
+OTHER = array(2, REST, N, N)
 SIDE = array(2, CX, RIM, N)
+RINGS = (array(2, CX, 8, N),) * RING
 
 
 PARAMS = pltpu.CompilerParams(vmem_limit_bytes=VMEM_LIMIT)
@@ -482,25 +474,31 @@
     )(*scalars, *operands, *later)
 
 
-def prepare(place, coupling_x, coupling_y, planes, z_table, y_table):
+HBM = pl.BlockSpec(memory_space=pltpu.HBM)
+
+
+def prepare(place, coupling_x, coupling_y, field, forward, inverse, after):
+    table = jax.ShapeDtypeStruct((2, 2 * N, 2 * N), BF)
     return pl.pallas_call(
         spectrum_kernel,
-        in_specs=[SMEM] * 3 + [WHOLE] * 3,
-        out_specs=(SMEM, SMEM, WHOLE, WHOLE),
-        out_shape=(array(2 * RIM, RIM), array(RIM, RIM), array(2, RIM, RIM, N), PART),
+        in_specs=[SMEM] * 3 + [HBM] + [WHOLE] * 2 + [pl.BlockSpec(memory_space=pl.ANY)],
+        out_specs=(SMEM,) * 2 + (WHOLE,) * 4,
+        out_shape=(
+            array(2 * RIM, RIM), array(RIM, RIM), array(2, RIM, RIM, N), OTHER, table, table
+        ),
+        scratch_shapes=[pltpu.VMEM(OTHER.shape, F32), pltpu.SemaphoreType.DMA],
         compiler_params=PARAMS,
         cost_estimate=COST,
-    )(place, coupling_x, coupling_y, planes, z_table, y_table)
+    )(place, coupling_x, coupling_y, field, forward, inverse, after)
 
 
 def cut_faces(place, field):
-    out = (SIDE, PART, FACE, PART)
     return pl.pallas_call(
         cut_kernel,
-        in_specs=[SMEM, pl.BlockSpec(memory_space=pltpu.HBM)],
-        out_specs=(WHOLE,) * 4,
-        out_shape=out,
-        scratch_shapes=[pltpu.SemaphoreType.DMA((4,))],
+        in_specs=[SMEM, HBM],
+        out_specs=(WHOLE,) * 3,
+        out_shape=(SIDE, PART, FACE),
+        scratch_shapes=[pltpu.SemaphoreType.DMA((3,))],
         compiler_params=PARAMS,
         cost_estimate=COST,
     )(place, field)
@@ -516,17 +514,19 @@
     far_pairs = [(i, ((i + 1) ^ 1) - 1) for i in range(1, n_gx - 1)]
     side_pairs = [(i, i ^ 1) for i in range(n_gy)]
 
-    zf, zi, yf, yi = (jnp.asarray(t) for t in dft_tables())
+    forward, inverse = (jnp.asarray(t, F32) for t in dft_tables())
     green = jnp.asarray(green_table())
     lines = jnp.asarray(green_lines())
 
-    weights = jnp.stack([odd, 1 - odd]).astype(F32)
+    weights = jnp.stack([odd, 1 - odd, gy, 1 - gy]).astype(F32)
     span = CX - RIM
     place = jnp.stack([odd * span, (1 - odd) * span, (1 - gy) * (N - RIM), 1 - gy]).astype(jnp.int32)
-    rims = side_tables(dft_tables()[2])
-
-    side_out, first_out, near_out, second_raw = cut_faces(place, field)
-    mix_x, mix_far, mix_y, second_out = prepare(place, coupling_x, coupling_y, second_raw, zf, yf)
+    pinned = pltpu.with_memory_space_constraint(field, pltpu.HBM)
+    side_out, first_out, near_out = cut_faces(place, pinned)
+    mix_x, mix_far, mix_y, second_out, zf, zi = prepare(
+        place, coupling_x, coupling_y, pinned, forward, inverse, first_out
+    )
+    yf, yi = zi, zf
     for step in range(2):
         side_in = lax.ppermute(side_out, "gy", side_pairs)
         first_in = lax.ppermute(first_out, "gx", far_pairs)
@@ -536,17 +536,17 @@
 
         def far_part(after):
             return call(
-                first_kernel, (mix_far,), (first_in, zf, yf), FACE, after=after,
-                weight=10 if step == 0 else 60,
+                first_kernel, (mix_far,), (first_in, zf, yf), FACE, after=after, weight=60
             )
 
         first = far_part(place) if step == 1 else None
         hat = call(
-            local_kernel, (weights, mix_x), (mix_y, field, source, wave, near_in, zf, yf), VOLUME,
-            after=place if first is None else first, weight=5,
+            local_kernel, (weights, place, mix_x), (mix_y, field, source, wave, near_in, zf), VOLUME,
+            after=place if first is None else first,
         )
         part = call(
-            side_kernel, (place,), (mix_y, side_in, hat, zf, rims, green), VOLUME, (rows, rows), weight=30
+            side_kernel, (weights, place), (mix_y, side_in, hat, zf, yf, green), VOLUME, (rows, rows),
+            weight=30,
         )
         if first is None:
             first = far_part(part)
@@ -557,7 +557,7 @@
             )
             field, side_out, near_out, second_out = call(
                 middle_kernel, (place,), (whole, part, green, field, wave, yi, zi, zf, yf),
-                (VOLUME, SIDE, FACE, PART), (VOLUME,),
+                (VOLUME, SIDE, FACE, OTHER), (VOLUME, *RINGS),
             )
         else:
             field = pl.pallas_call(
@@ -568,7 +568,8 @@
                 scratch_shapes=[
                     pltpu.VMEM(VOLUME.shape, F32),
                     pltpu.VMEM(VOLUME.shape, F32),
-                    pltpu.SemaphoreType.DMA((3,)),
+                    pltpu.SemaphoreType.DMA((CX // RIM,)),
+                    *(pltpu.VMEM(r.shape, F32) for r in RINGS),
                 ],
                 compiler_params=PARAMS,
                 cost_estimate=COST,

time: 93.6 us -> 87.5 us (0.935)
  the two profiles are of different devices: /device:TPU:1 before, /device:TPU:24 now
where the time goes in v2:
time: 87.5 us; the launch traced here: 87.2 us
  Pallas kernels  57.3 us (65%)
  starting transfers between devices  21.5 us (25%)
  waiting for transfers between devices  5.55 us (6%)
  local copies, waits for them, and re-layouts  2.22 us (3%)
    pallas_call x8, Pallas kernels, call(): pl.pallas_call(kernel, in_specs=[SMEM] * len(scalars) + [WHOLE] * len(ope...  42.3 us
    ppermute x2, starting transfers between devices, body(): first_in = lax.ppermute(first_out, 'gx', far_pairs)  10.1 us
    pallas_call x1, Pallas kernels, body(): pl.pallas_call(last_kernel, in_specs=[SMEM] * 2 + [WHOLE] * 8, out_specs=...  9.59 us
    ppermute x2, starting transfers between devices, body(): second_in = lax.ppermute(second_out, 'gx', far_pairs)  5.9 us
    ppermute x2, waiting for transfers between devices, body(): side_in = lax.ppermute(side_out, 'gy', side_pairs)  5.48 us
    ppermute x2, starting transfers between devices, body(): side_in = lax.ppermute(side_out, 'gy', side_pairs)  5.18 us
    pallas_call x1, Pallas kernels, prepare(): pl.pallas_call(spectrum_kernel, in_specs=[SMEM] * 3 + [HBM] + [WHOLE] * 2...  3.05 us
    pallas_call x1, Pallas kernels, cut_faces(): pl.pallas_call(cut_kernel, in_specs=[SMEM, HBM], out_specs=(WHOLE,) * 3,...  2.33 us
  transfers between devices with their start and end apart: 8, of which 2 were waited for; matrix products, arithmetic and copies ran while one was open for 0% of the time, Pallas kernels for 49%

profile of v2, /device:TPU:24, one launch (start us, length us, event | category | flops | bytes accessed | tf_op | source)
XLA Modules:
  0.0 87.2 jit_solution(17784158633923716260)
XLA Ops:
  0.0 0.1 add_add_fusion.place_ref.after_ref
  0.1 2.3 %shard_map.91 = (f32[2,32,8,128]{3,2,1,0:T(8,128)S(1)}, f32[2,3,128,128]{3,2,1,0:T(8,128)S(1)}, f32[2,8,128,128]{3,2,1,0:T(8,128)S(1)}) custom-call(s32[4]{0:T(128)S(1)} %add_add_fusion.place_ref.after_ref, f32[2,32,128,128]{3,2,1,0:T(8,128)} %field_ref.9), custom_call_target="tpu_custom_call" | custom-call | flops 1000000000 | bytes 1000000 | tf_op jit(solution)/shard_map/pallas_call | solution.py:496
  2.5 0.1 collective-permute-start.3
  2.6 4.0 %collective-permute-start.2 = (f32[2,32,8,128]{3,2,1,0:T(8,128)S(1)}, f32[2,32,8,128]{3,2,1,0:T(8,128)S(1)}, u32[]{:S(2)}, u32[]{:S(2)}) collective-permute-start(f32[2,32,8,128]{3,2,1,0:T(8,128)S(1)} %get-tuple-element.26), channel_id=1, source_target_pairs={{0,1},{1,0},{2,3},{3,2},{4,5},{5,4},{6,7},{7,6},{8,9},{9,8},{10,11... | collective-permute-start | bytes 786440 | tf_op jit(solution)/shard_map/ppermute | solution.py:531
  6.5 5.0 %collective-permute-start.1 = (f32[2,3,128,128]{3,2,1,0:T(8,128)S(1)}, f32[2,3,128,128]{3,2,1,0:T(8,128)S(1)}, u32[]{:S(2)}, u32[]{:S(2)}) collective-permute-start(f32[2,3,128,128]{3,2,1,0:T(8,128)S(1)} %get-tuple-element.20.after_ref), channel_id=1, source_target_pairs={{2,4},{4,2},{6,8},{8,6},{10,12},{12,10},{14,16},{16,14},{18,20},{2... | collective-permute-start | bytes 1179656 | tf_op jit(solution)/shard_map/ppermute | solution.py:532
  11.6 3.0 %shard_map.92 = (f32[16,8]{1,0:T(8,128)S(1)}, f32[8,8]{1,0:T(8,128)S(1)}, f32[2,8,8,128]{3,2,1,0:T(8,128)S(1)}, f32[2,5,128,128]{3,2,1,0:T(8,128)S(1)}, bf16[2,2...) custom-call(s32[4]{0:T(128)S(1)} %add_add_fusion.place_ref.after_ref, f32[8,8]{1,0:T(8,128)S(1)} %copy-done.8, ...), custom_call_target="tpu_custom_call" | custom-call | flops 1000000000 | bytes 1000000 | tf_op jit(solution)/shard_map/pallas_call | solution.py:482
  14.7 3.5 %collective-permute-start = (f32[2,5,128,128]{3,2,1,0:T(8,128)S(1)}, f32[2,5,128,128]{3,2,1,0:T(8,128)S(1)}, u32[]{:S(2)}, u32[]{:S(2)}) collective-permute-start(f32[2,5,128,128]{3,2,1,0:T(8,128)S(1)} %get-tuple-element.22), channel_id=1, source_target_pairs={{2,4},{4,2},{6,8},{8,6},{10,12},{12,10},{14,16},{16,14},{18,20},{2... | collective-permute-start | bytes 1966088 | tf_op jit(solution)/shard_map/ppermute | solution.py:534
  18.2 0.1 add_convert_fusion.side_ref
  18.3 0.0 collective-permute-done.3.near_ref
  18.3 0.0 copy-start.2
  18.3 2.2 %copy-done.2 = f32[2,32,128,128]{3,2,1,0:T(8,128)S(1)} copy-done((f32[2,32,128,128]{3,2,1,0:T(8,128)S(1)}, f32[2,32,128,128]{3,2,1,0:T(8,128)}, u32[]{:S(2)}) %copy-start.2) | copy-done | bytes 4194328
  20.5 5.8 %shard_map.93.hat_ref = f32[2,32,128,128]{3,2,1,0:T(8,128)S(1)} custom-call(f32[4]{0:T(128)S(1)} %add_convert_fusion.side_ref, s32[4]{0:T(128)S(1)} %add_add_fusion.place_ref.after_ref, f32[16,8]{1,0:T(8,128)S(1)} %get-tuple-element.27.mix_x_ref, f32[2,8,8,128]{3,2,1,0:T(8,128)S(1)} %get-tuple-element.25.mix_y_ref, f32[2,32,128,128]{3,2,1,0:T(8,128)S(1)} %copy-done, ...), custom_call_target="tpu_custom_call" | custom-call | flops 1000000000 | bytes 1000000 | tf_op jit(solution)/shard_map/pallas_call | solution.py:465
  26.3 0.0 collective-permute-done.2.face_ref
  26.3 6.8 %shard_map.94.after_ref.part_ref = f32[2,32,128,128]{3,2,1,0:T(8,128)S(1)} custom-call(f32[4]{0:T(128)S(1)} %add_convert_fusion.side_ref, s32[4]{0:T(128)S(1)} %add_add_fusion.place_ref.after_ref, f32[2,8,8,128]{3,2,1,0:T(8,128)S(1)} %get-tuple-element.25.mix_y_ref, f32[2,32,8,128]{3,2,1,0:T(8,128)S(1)} %collective-permute-done.2.face_ref, ...), custom_call_target="tpu_custom_call" | custom-call | flops 30000001024 | bytes 30000000 | tf_op jit(solution)/shard_map/pallas_call | solution.py:465
  33.1 0.0 collective-permute-done.1.face_ref
  33.1 0.0 copy-start.5
  33.1 2.6 %shard_map.95.first_ref = f32[2,8,128,128]{3,2,1,0:T(8,128)S(1)} custom-call(f32[8,8]{1,0:T(8,128)S(1)} %get-tuple-element.21.mix_ref, f32[2,3,128,128]{3,2,1,0:T(8,128)S(1)} %collective-permute-done.1.face_ref, bf16[2,256,256]{2,1,0:T(8,128)(2,1)S(1)} %get-tuple-element.23.z_ref.y_ref.yi_ref, bf16[2,256,256]{2,1,0:T(8,128)(2,1)S(1)} %get-tuple-element.24.y_ref.z_ref.zi_ref, ...), custom_call_target="tpu_custom_call" | custom-call | flops 60000002048 | bytes 60000000 | tf_op jit(solution)/shard_map/pallas_call | solution.py:465
  35.7 2.7 %shard_map.96 = (f32[2,8,128,128]{3,2,1,0:T(8,128)S(1)}, f32[2,3,128,128]{3,2,1,0:T(8,128)S(1)}) custom-call(s32[4]{0:T(128)S(1)} %add_add_fusion.place_ref.after_ref, f32[8,8]{1,0:T(8,128)S(1)} %get-tuple-element.21.mix_ref, f32[2,5,128,128]{3,2,1,0:T(8,128)S(1)} %collective-permute-done.second_ref, f32[2,8,128,128]{3,2,1,0:T(8,128)S(1)} %shard_map.95.first_ref, ...), custom_call_target="tpu_custom_call" | custom-call | flops 1000000000 | bytes 1000000 | tf_op jit(solution)/shard_map/pallas_call | solution.py:465
  38.4 5.1 %collective-permute-start.5 = (f32[2,3,128,128]{3,2,1,0:T(8,128)S(1)}, f32[2,3,128,128]{3,2,1,0:T(8,128)S(1)}, u32[]{:S(2)}, u32[]{:S(2)}) collective-permute-start(f32[2,3,128,128]{3,2,1,0:T(8,128)S(1)} %get-tuple-element.31), channel_id=1, source_target_pairs={{2,4},{4,2},{6,8},{8,6},{10,12},{12,10},{14,16},{16,14},{18,20},{2... | collective-permute-start | bytes 1179656 | tf_op jit(solution)/shard_map/ppermute | solution.py:532
  43.4 9.3 %shard_map.97 = (f32[2,32,128,128]{3,2,1,0:T(8,128)S(1)}, f32[2,32,8,128]{3,2,1,0:T(8,128)S(1)}, f32[2,8,128,128]{3,2,1,0:T(8,128)S(1)}, f32[2,5,128,128]{3,2,1,0:T(8,128)S(1)}) custom-call(s32[4]{0:T(128)S(1)} %add_add_fusion.place_ref.after_ref, f32[2,8,128,128]{3,2,1,0:T(8,128)S(1)} %get-tuple-element.29.hat_ref, ...), custom_call_target="tpu_custom_call" | custom-call | flops 1000000000 | bytes 1000000 | tf_op jit(solution)/shard_map/pallas_call | solution.py:465
  52.8 1.2 %collective-permute-start.6 = (f32[2,32,8,128]{3,2,1,0:T(8,128)S(1)}, f32[2,32,8,128]{3,2,1,0:T(8,128)S(1)}, u32[]{:S(2)}, u32[]{:S(2)}) collective-permute-start(f32[2,32,8,128]{3,2,1,0:T(8,128)S(1)} %get-tuple-element.32), channel_id=1, source_target_pairs={{0,1},{1,0},{2,3},{3,2},{4,5},{5,4},{6,7},{7,6},{8,9},{9,8},{10,11... | collective-permute-start | bytes 786440 | tf_op jit(solution)/shard_map/ppermute | solution.py:531
  54.0 2.4 %collective-permute-start.4 = (f32[2,5,128,128]{3,2,1,0:T(8,128)S(1)}, f32[2,5,128,128]{3,2,1,0:T(8,128)S(1)}, u32[]{:S(2)}, u32[]{:S(2)}) collective-permute-start(f32[2,5,128,128]{3,2,1,0:T(8,128)S(1)} %get-tuple-element.30), channel_id=1, source_target_pairs={{2,4},{4,2},{6,8},{8,6},{10,12},{12,10},{14,16},{16,14},{18,20},{2... | collective-permute-start | bytes 1966088 | tf_op jit(solution)/shard_map/ppermute | solution.py:534
  56.4 0.0 copy-start.3
  56.4 0.3 collective-permute-start.7
  56.7 0.0 collective-permute-done.5.face_ref
  56.7 2.6 %shard_map.98.after_ref.first_ref = f32[2,8,128,128]{3,2,1,0:T(8,128)S(1)} custom-call(f32[8,8]{1,0:T(8,128)S(1)} %get-tuple-element.21.mix_ref, f32[2,3,128,128]{3,2,1,0:T(8,128)S(1)} %collective-permute-done.5.face_ref, bf16[2,256,256]{2,1,0:T(8,128)(2,1)S(1)} %get-tuple-element.23.z_ref.y_ref.yi_ref, ...), custom_call_target="tpu_custom_call" | custom-call | flops 60000002048 | bytes 60000000 | tf_op jit(solution)/shard_map/pallas_call | solution.py:465
  59.3 0.1 collective-permute-done.7.near_ref
  59.3 5.8 %shard_map.99.hat_ref = f32[2,32,128,128]{3,2,1,0:T(8,128)S(1)} custom-call(f32[4]{0:T(128)S(1)} %add_convert_fusion.side_ref, s32[4]{0:T(128)S(1)} %add_add_fusion.place_ref.after_ref, f32[16,8]{1,0:T(8,128)S(1)} %get-tuple-element.27.mix_x_ref, f32[2,8,8,128]{3,2,1,0:T(8,128)S(1)} %get-tuple-element.25.mix_y_ref, ...), custom_call_target="tpu_custom_call" | custom-call | flops 1000000000 | bytes 1000000 | tf_op jit(solution)/shard_map/pallas_call | solution.py:465
  65.2 5.5 %collective-permute-done.6.face_ref = f32[2,32,8,128]{3,2,1,0:T(8,128)S(1)} collective-permute-done((f32[2,32,8,128]{3,2,1,0:T(8,128)S(1)}, f32[2,32,8,128]{3,2,1,0:T(8,128)S(1)}, u32[]{:S(2)}, u32[]{:S(2)}) %collective-permute-start.6) | collective-permute-done | bytes 262176 | tf_op jit(solution)/shard_map/ppermute | solution.py:531
  70.6 6.8 %shard_map.100.part_ref = f32[2,32,128,128]{3,2,1,0:T(8,128)S(1)} custom-call(f32[4]{0:T(128)S(1)} %add_convert_fusion.side_ref, s32[4]{0:T(128)S(1)} %add_add_fusion.place_ref.after_ref, f32[2,8,8,128]{3,2,1,0:T(8,128)S(1)} %get-tuple-element.25.mix_y_ref, f32[2,32,8,128]{3,2,1,0:T(8,128)S(1)} %collective-permute-done.6.face_ref, ...), custom_call_target="tpu_custom_call" | custom-call | flops 30000001024 | bytes 30000000 | tf_op jit(solution)/shard_map/pallas_call | solution.py:465
  77.4 0.0 collective-permute-done.4.second_ref
  77.4 9.6 %shard_map.101 = f32[2,32,128,128]{3,2,1,0:T(8,128)} custom-call(s32[4]{0:T(128)S(1)} %add_add_fusion.place_ref.after_ref, f32[8,8]{1,0:T(8,128)S(1)} %get-tuple-element.21.mix_ref, f32[2,5,128,128]{3,2,1,0:T(8,128)S(1)} %collective-permute-done.4.second_ref, f32[2,8,128,128]{3,2,1,0:T(8,128)S(1)} %shard_map.98.after_ref.first_ref, ...), custom_call_target="tpu_custom_call" | custom-call | flops 1000000000 | bytes 1000000 | tf_op jit(solution)/shard_map/pallas_call | solution.py:563
  (17 shorter events, 0.0 us)
Async XLA Ops:
  0.0 11.6 %copy-start.6 = (f32[256,256]{1,0:T(8,128)S(1)}, f32[256,256]{1,0:T(8,128)}, u32[]{:S(2)}) copy-start(f32[256,256]{1,0:T(8,128)} %constant.35.clone.inverse_ref) | copy-start | bytes 786436
  0.0 11.6 %copy-start.7 = (f32[256,256]{1,0:T(8,128)S(1)}, f32[256,256]{1,0:T(8,128)}, u32[]{:S(2)}) copy-start(f32[256,256]{1,0:T(8,128)} %constant.34.clone.forward_ref) | copy-start | bytes 786436
  0.0 11.6 %copy-start.9 = (f32[8,8]{1,0:T(8,128)S(1)}, f32[8,8]{1,0:T(8,128)}, u32[]{:S(2)}) copy-start(f32[8,8]{1,0:T(8,128)} %y_coupling_ref.1) | copy-start | bytes 772
  0.0 11.6 %copy-start.8 = (f32[8,8]{1,0:T(8,128)S(1)}, f32[8,8]{1,0:T(8,128)}, u32[]{:S(2)}) copy-start(f32[8,8]{1,0:T(8,128)} %x_ref.1) | copy-start | bytes 772
  0.1 18.1 %copy-start = (f32[2,32,128,128]{3,2,1,0:T(8,128)S(1)}, f32[2,32,128,128]{3,2,1,0:T(8,128)}, u32[]{:S(2)}) copy-start(f32[2,32,128,128]{3,2,1,0:T(8,128)} %field_ref.9) | copy-start | bytes 12582916
  0.1 18.1 %copy-start.1 = (f32[32,128,128]{2,1,0:T(8,128)S(1)}, f32[32,128,128]{2,1,0:T(8,128)}, u32[]{:S(2)}) copy-start(f32[32,128,128]{2,1,0:T(8,128)} %wave_ref.9) | copy-start | bytes 6291460
  2.5 15.8 %collective-permute-start.3 = (f32[2,8,128,128]{3,2,1,0:T(8,128)S(1)}, f32[2,8,128,128]{3,2,1,0:T(8,128)S(1)}, u32[]{:S(2)}, u32[]{:S(2)}) collective-permute-start(f32[2,8,128,128]{3,2,1,0:T(8,128)S(1)} %get-tuple-element.28), channel_id=1, source_target_pairs={{0,2},{2,0},{4,6},{6,4},{8,10},{10,8},{12,14},{14,12},{16,18},{18,... | collective-permute-start | bytes 3145736 | tf_op jit(solution)/shard_map/ppermute | solution.py:533
  2.6 23.7 %collective-permute-start.2 = (f32[2,32,8,128]{3,2,1,0:T(8,128)S(1)}, f32[2,32,8,128]{3,2,1,0:T(8,128)S(1)}, u32[]{:S(2)}, u32[]{:S(2)}) collective-permute-start(f32[2,32,8,128]{3,2,1,0:T(8,128)S(1)} %get-tuple-element.26), channel_id=1, source_target_pairs={{0,1},{1,0},{2,3},{3,2},{4,5},{5,4},{6,7},{7,6},{8,9},{9,8},{10,11... | collective-permute-start | bytes 786440 | tf_op jit(solution)/shard_map/ppermute | solution.py:531
  6.5 26.6 %collective-permute-start.1 = (f32[2,3,128,128]{3,2,1,0:T(8,128)S(1)}, f32[2,3,128,128]{3,2,1,0:T(8,128)S(1)}, u32[]{:S(2)}, u32[]{:S(2)}) collective-permute-start(f32[2,3,128,128]{3,2,1,0:T(8,128)S(1)} %get-tuple-element.20.after_ref), channel_id=1, source_target_pairs={{2,4},{4,2},{6,8},{8,6},{10,12},{12,10},{14,16},{16,14},{18,20},{2... | collective-permute-start | bytes 1179656 | tf_op jit(solution)/shard_map/ppermute | solution.py:532
  14.7 21.0 %collective-permute-start = (f32[2,5,128,128]{3,2,1,0:T(8,128)S(1)}, f32[2,5,128,128]{3,2,1,0:T(8,128)S(1)}, u32[]{:S(2)}, u32[]{:S(2)}) collective-permute-start(f32[2,5,128,128]{3,2,1,0:T(8,128)S(1)} %get-tuple-element.22), channel_id=1, source_target_pairs={{2,4},{4,2},{6,8},{8,6},{10,12},{12,10},{14,16},{16,14},{18,20},{2... | collective-permute-start | bytes 1966088 | tf_op jit(solution)/shard_map/ppermute | solution.py:534
  18.3 2.2 %copy-start.2 = (f32[2,32,128,128]{3,2,1,0:T(8,128)S(1)}, f32[2,32,128,128]{3,2,1,0:T(8,128)}, u32[]{:S(2)}) copy-start(f32[2,32,128,128]{3,2,1,0:T(8,128)} %source_ref.3) | copy-start | bytes 12582916
  20.5 5.8 %copy-start.4 = (f32[17,2,128,128]{3,2,1,0:T(8,128)S(1)}, f32[17,2,128,128]{3,2,1,0:T(8,128)}, u32[]{:S(2)}) copy-start(f32[17,2,128,128]{3,2,1,0:T(8,128)} %constant.36.clone.green_ref) | copy-start | bytes 6684676
  33.1 2.6 %copy-start.5 = (f32[8,2,128,128]{3,2,1,0:T(8,128)S(1)}, f32[8,2,128,128]{3,2,1,0:T(8,128)}, u32[]{:S(2)}) copy-start(f32[8,2,128,128]{3,2,1,0:T(8,128)} %constant.37.clone.line_ref) | copy-start | bytes 3145732
  38.4 18.3 %collective-permute-start.5 = (f32[2,3,128,128]{3,2,1,0:T(8,128)S(1)}, f32[2,3,128,128]{3,2,1,0:T(8,128)S(1)}, u32[]{:S(2)}, u32[]{:S(2)}) collective-permute-start(f32[2,3,128,128]{3,2,1,0:T(8,128)S(1)} %get-tuple-element.31), channel_id=1, source_target_pairs={{2,4},{4,2},{6,8},{8,6},{10,12},{12,10},{14,16},{16,14},{18,20},{2... | collective-permute-start | bytes 1179656 | tf_op jit(solution)/shard_map/ppermute | solution.py:532
  52.8 17.9 %collective-permute-start.6 = (f32[2,32,8,128]{3,2,1,0:T(8,128)S(1)}, f32[2,32,8,128]{3,2,1,0:T(8,128)S(1)}, u32[]{:S(2)}, u32[]{:S(2)}) collective-permute-start(f32[2,32,8,128]{3,2,1,0:T(8,128)S(1)} %get-tuple-element.32), channel_id=1, source_target_pairs={{0,1},{1,0},{2,3},{3,2},{4,5},{5,4},{6,7},{7,6},{8,9},{9,8},{10,11... | collective-permute-start | bytes 786440 | tf_op jit(solution)/shard_map/ppermute | solution.py:531
  54.0 23.4 %collective-permute-start.4 = (f32[2,5,128,128]{3,2,1,0:T(8,128)S(1)}, f32[2,5,128,128]{3,2,1,0:T(8,128)S(1)}, u32[]{:S(2)}, u32[]{:S(2)}) collective-permute-start(f32[2,5,128,128]{3,2,1,0:T(8,128)S(1)} %get-tuple-element.30), channel_id=1, source_target_pairs={{2,4},{4,2},{6,8},{8,6},{10,12},{12,10},{14,16},{16,14},{18,20},{2... | collective-permute-start | bytes 1966088 | tf_op jit(solution)/shard_map/ppermute | solution.py:534
  56.4 2.9 %copy-start.3 = (f32[2,32,128,128]{3,2,1,0:T(8,128)S(1)}, f32[2,32,128,128]{3,2,1,0:T(8,128)}, u32[]{:S(2)}) copy-start(f32[2,32,128,128]{3,2,1,0:T(8,128)} %source_ref.3) | copy-start | bytes 12582916
  56.4 2.9 %collective-permute-start.7 = (f32[2,8,128,128]{3,2,1,0:T(8,128)S(1)}, f32[2,8,128,128]{3,2,1,0:T(8,128)S(1)}, u32[]{:S(2)}, u32[]{:S(2)}) collective-permute-start(f32[2,8,128,128]{3,2,1,0:T(8,128)S(1)} %get-tuple-element.34), channel_id=1, source_target_pairs={{0,2},{2,0},{4,6},{6,4},{8,10},{10,8},{12,14},{14,12},{16,18},{18,... | collective-permute-start | bytes 3145736 | tf_op jit(solution)/shard_map/ppermute | solution.py:533

commit v3 on v2

--- a/solution.py
+++ b/solution.py
@@ -12,7 +12,7 @@
 RIM = 8
 LEAD = 3
 REST = RIM - LEAD
-RING = 4
+RING = 8
 K0SQ = 2.4674
 EPS = 2.5
 CX = 32
@@ -318,9 +318,8 @@
 
 
 def damped(re, im, back, wave):
-    ratio = (wave - K0SQ) * (1.0 / EPS)
-    r_re, r_im = re - back[0], im - back[1]
-    return re - (r_re - ratio * r_im), im - (r_im + ratio * r_re)
+    ratio = wave * (1.0 / EPS) - K0SQ / EPS
+    return back[0] + ratio * (im - back[1]), back[1] - ratio * (re - back[0])
 
 
 def early_kernel(
@@ -331,21 +330,19 @@
 
     @tiles(N, 8)
     def _(rows):
+        given = []
         for part in range(2):
             source = [second_ref[part, r, rows, :] for r in range(REST)]
-            for p in range(RIM):
-                hat_ref[part, p, rows, :] = first_ref[part, p, rows, :] - mixed(
-                    mix_ref, p, LEAD, source
-                )
-
-    @tiles(N, 8)
-    def _(rows):
-        given = [(hat_ref[0, p, rows, :], hat_ref[1, p, rows, :]) for p in range(RIM)]
+            given.append(
+                [first_ref[part, p, rows, :] - mixed(mix_ref, p, LEAD, source) for p in range(RIM)]
+            )
+            for p, value in enumerate(given[part]):
+                hat_ref[part, p, rows, :] = value
         lines = [(line_ref[d, 0, rows, :], line_ref[d, 1, rows, :]) for d in range(RIM)]
         for p in range(LEAD):
             re = part_ref[0, p, rows, :]
             im = part_ref[1, p, rows, :]
-            for q, (t_re, t_im) in enumerate(given):
+            for q, (t_re, t_im) in enumerate(zip(*given)):
                 g_re, g_im = lines[abs(p - q)]
                 re += t_re * g_re - t_im * g_im
                 im += t_re * g_im + t_im * g_re

time: 87.5 us -> 85.6 us (0.978)
  Pallas kernels: 57.3 us -> 55.5 us
    pallas_call x8, Pallas kernels: 42.3 us -> 41.3 us  [call(): pl.pallas_call(kernel, in_specs=[SMEM] * len(scalars) + [WHOLE] * len(ope...]
where the time goes in v3:
time: 85.6 us; the launch traced here: 85.3 us
  Pallas kernels  55.5 us (65%)
  starting transfers between devices  21.5 us (25%)
  waiting for transfers between devices  5.54 us (6%)
  local copies, waits for them, and re-layouts  2.22 us (3%)
    pallas_call x8, Pallas kernels, call(): pl.pallas_call(kernel, in_specs=[SMEM] * len(scalars) + [WHOLE] * len(ope...  41.3 us
    ppermute x2, starting transfers between devices, body(): first_in = lax.ppermute(first_out, 'gx', far_pairs)  10.1 us
    pallas_call x1, Pallas kernels, body(): pl.pallas_call(last_kernel, in_specs=[SMEM] * 2 + [WHOLE] * 8, out_specs=...  8.79 us
    ppermute x2, starting transfers between devices, body(): second_in = lax.ppermute(second_out, 'gx', far_pairs)  5.9 us
    ppermute x2, waiting for transfers between devices, body(): side_in = lax.ppermute(side_out, 'gy', side_pairs)  5.47 us
    ppermute x2, starting transfers between devices, body(): side_in = lax.ppermute(side_out, 'gy', side_pairs)  5.18 us
    pallas_call x1, Pallas kernels, prepare(): pl.pallas_call(spectrum_kernel, in_specs=[SMEM] * 3 + [HBM] + [WHOLE] * 2...  3.05 us
    pallas_call x1, Pallas kernels, cut_faces(): pl.pallas_call(cut_kernel, in_specs=[SMEM, HBM], out_specs=(WHOLE,) * 3,...  2.33 us
  transfers between devices with their start and end apart: 8, of which 2 were waited for; matrix products, arithmetic and copies ran while one was open for 0% of the time, Pallas kernels for 49%

profile of v3, /device:TPU:24, one launch (start us, length us, event | category | flops | bytes accessed | tf_op | source)
XLA Modules:
  0.0 85.3 jit_solution(13450459778661650530)
XLA Ops:
  0.0 0.1 add_add_fusion.place_ref.after_ref
  0.1 2.3 %shard_map.91 = (f32[2,32,8,128]{3,2,1,0:T(8,128)S(1)}, f32[2,3,128,128]{3,2,1,0:T(8,128)S(1)}, f32[2,8,128,128]{3,2,1,0:T(8,128)S(1)}) custom-call(s32[4]{0:T(128)S(1)} %add_add_fusion.place_ref.after_ref, f32[2,32,128,128]{3,2,1,0:T(8,128)} %field_ref.9), custom_call_target="tpu_custom_call" | custom-call | flops 1000000000 | bytes 1000000 | tf_op jit(solution)/shard_map/pallas_call | solution.py:493
  2.5 0.1 collective-permute-start.3
  2.6 4.0 %collective-permute-start.2 = (f32[2,32,8,128]{3,2,1,0:T(8,128)S(1)}, f32[2,32,8,128]{3,2,1,0:T(8,128)S(1)}, u32[]{:S(2)}, u32[]{:S(2)}) collective-permute-start(f32[2,32,8,128]{3,2,1,0:T(8,128)S(1)} %get-tuple-element.26), channel_id=1, source_target_pairs={{0,1},{1,0},{2,3},{3,2},{4,5},{5,4},{6,7},{7,6},{8,9},{9,8},{10,11... | collective-permute-start | bytes 786440 | tf_op jit(solution)/shard_map/ppermute | solution.py:528
  6.5 5.0 %collective-permute-start.1 = (f32[2,3,128,128]{3,2,1,0:T(8,128)S(1)}, f32[2,3,128,128]{3,2,1,0:T(8,128)S(1)}, u32[]{:S(2)}, u32[]{:S(2)}) collective-permute-start(f32[2,3,128,128]{3,2,1,0:T(8,128)S(1)} %get-tuple-element.20.after_ref), channel_id=1, source_target_pairs={{2,4},{4,2},{6,8},{8,6},{10,12},{12,10},{14,16},{16,14},{18,20},{2... | collective-permute-start | bytes 1179656 | tf_op jit(solution)/shard_map/ppermute | solution.py:529
  11.6 3.0 %shard_map.92 = (f32[16,8]{1,0:T(8,128)S(1)}, f32[8,8]{1,0:T(8,128)S(1)}, f32[2,8,8,128]{3,2,1,0:T(8,128)S(1)}, f32[2,5,128,128]{3,2,1,0:T(8,128)S(1)}, bf16[2,2...) custom-call(s32[4]{0:T(128)S(1)} %add_add_fusion.place_ref.after_ref, f32[8,8]{1,0:T(8,128)S(1)} %copy-done.8, ...), custom_call_target="tpu_custom_call" | custom-call | flops 1000000000 | bytes 1000000 | tf_op jit(solution)/shard_map/pallas_call | solution.py:479
  14.7 3.5 %collective-permute-start = (f32[2,5,128,128]{3,2,1,0:T(8,128)S(1)}, f32[2,5,128,128]{3,2,1,0:T(8,128)S(1)}, u32[]{:S(2)}, u32[]{:S(2)}) collective-permute-start(f32[2,5,128,128]{3,2,1,0:T(8,128)S(1)} %get-tuple-element.22), channel_id=1, source_target_pairs={{2,4},{4,2},{6,8},{8,6},{10,12},{12,10},{14,16},{16,14},{18,20},{2... | collective-permute-start | bytes 1966088 | tf_op jit(solution)/shard_map/ppermute | solution.py:531
  18.2 0.1 add_convert_fusion.side_ref
  18.3 0.0 collective-permute-done.3.near_ref
  18.3 0.0 copy-start.2
  18.3 2.2 %copy-done.2 = f32[2,32,128,128]{3,2,1,0:T(8,128)S(1)} copy-done((f32[2,32,128,128]{3,2,1,0:T(8,128)S(1)}, f32[2,32,128,128]{3,2,1,0:T(8,128)}, u32[]{:S(2)}) %copy-start.2) | copy-done | bytes 4194328
  20.5 5.8 %shard_map.93.hat_ref = f32[2,32,128,128]{3,2,1,0:T(8,128)S(1)} custom-call(f32[4]{0:T(128)S(1)} %add_convert_fusion.side_ref, s32[4]{0:T(128)S(1)} %add_add_fusion.place_ref.after_ref, f32[16,8]{1,0:T(8,128)S(1)} %get-tuple-element.27.mix_x_ref, f32[2,8,8,128]{3,2,1,0:T(8,128)S(1)} %get-tuple-element.25.mix_y_ref, f32[2,32,128,128]{3,2,1,0:T(8,128)S(1)} %copy-done, ...), custom_call_target="tpu_custom_call" | custom-call | flops 1000000000 | bytes 1000000 | tf_op jit(solution)/shard_map/pallas_call | solution.py:462
  26.3 0.0 collective-permute-done.2.face_ref
  26.3 6.8 %shard_map.94.after_ref.part_ref = f32[2,32,128,128]{3,2,1,0:T(8,128)S(1)} custom-call(f32[4]{0:T(128)S(1)} %add_convert_fusion.side_ref, s32[4]{0:T(128)S(1)} %add_add_fusion.place_ref.after_ref, f32[2,8,8,128]{3,2,1,0:T(8,128)S(1)} %get-tuple-element.25.mix_y_ref, f32[2,32,8,128]{3,2,1,0:T(8,128)S(1)} %collective-permute-done.2.face_ref, ...), custom_call_target="tpu_custom_call" | custom-call | flops 30000001024 | bytes 30000000 | tf_op jit(solution)/shard_map/pallas_call | solution.py:462
  33.1 0.0 collective-permute-done.1.face_ref
  33.1 0.0 copy-start.5
  33.1 2.6 %shard_map.95.first_ref = f32[2,8,128,128]{3,2,1,0:T(8,128)S(1)} custom-call(f32[8,8]{1,0:T(8,128)S(1)} %get-tuple-element.21.mix_ref, f32[2,3,128,128]{3,2,1,0:T(8,128)S(1)} %collective-permute-done.1.face_ref, bf16[2,256,256]{2,1,0:T(8,128)(2,1)S(1)} %get-tuple-element.23.z_ref.y_ref.yi_ref, bf16[2,256,256]{2,1,0:T(8,128)(2,1)S(1)} %get-tuple-element.24.y_ref.z_ref.zi_ref, ...), custom_call_target="tpu_custom_call" | custom-call | flops 60000002048 | bytes 60000000 | tf_op jit(solution)/shard_map/pallas_call | solution.py:462
  35.7 0.0 collective-permute-done.second_ref
  35.7 2.3 %shard_map.96 = (f32[2,8,128,128]{3,2,1,0:T(8,128)S(1)}, f32[2,3,128,128]{3,2,1,0:T(8,128)S(1)}) custom-call(s32[4]{0:T(128)S(1)} %add_add_fusion.place_ref.after_ref, f32[8,8]{1,0:T(8,128)S(1)} %get-tuple-element.21.mix_ref, f32[2,5,128,128]{3,2,1,0:T(8,128)S(1)} %collective-permute-done.second_ref, f32[2,8,128,128]{3,2,1,0:T(8,128)S(1)} %shard_map.95.first_ref, ...), custom_call_target="tpu_custom_call" | custom-call | flops 1000000000 | bytes 1000000 | tf_op jit(solution)/shard_map/pallas_call | solution.py:462
  38.1 5.1 %collective-permute-start.5 = (f32[2,3,128,128]{3,2,1,0:T(8,128)S(1)}, f32[2,3,128,128]{3,2,1,0:T(8,128)S(1)}, u32[]{:S(2)}, u32[]{:S(2)}) collective-permute-start(f32[2,3,128,128]{3,2,1,0:T(8,128)S(1)} %get-tuple-element.31), channel_id=1, source_target_pairs={{2,4},{4,2},{6,8},{8,6},{10,12},{12,10},{14,16},{16,14},{18,20},{2... | collective-permute-start | bytes 1179656 | tf_op jit(solution)/shard_map/ppermute | solution.py:529
  43.1 8.6 %shard_map.97 = (f32[2,32,128,128]{3,2,1,0:T(8,128)S(1)}, f32[2,32,8,128]{3,2,1,0:T(8,128)S(1)}, f32[2,8,128,128]{3,2,1,0:T(8,128)S(1)}, f32[2,5,128,128]{3,2,1,0:T(8,128)S(1)}) custom-call(s32[4]{0:T(128)S(1)} %add_add_fusion.place_ref.after_ref, f32[2,8,128,128]{3,2,1,0:T(8,128)S(1)} %get-tuple-element.29.hat_ref, ...), custom_call_target="tpu_custom_call" | custom-call | flops 1000000000 | bytes 1000000 | tf_op jit(solution)/shard_map/pallas_call | solution.py:462
  51.8 1.2 %collective-permute-start.6 = (f32[2,32,8,128]{3,2,1,0:T(8,128)S(1)}, f32[2,32,8,128]{3,2,1,0:T(8,128)S(1)}, u32[]{:S(2)}, u32[]{:S(2)}) collective-permute-start(f32[2,32,8,128]{3,2,1,0:T(8,128)S(1)} %get-tuple-element.32), channel_id=1, source_target_pairs={{0,1},{1,0},{2,3},{3,2},{4,5},{5,4},{6,7},{7,6},{8,9},{9,8},{10,11... | collective-permute-start | bytes 786440 | tf_op jit(solution)/shard_map/ppermute | solution.py:528
  53.0 2.4 %collective-permute-start.4 = (f32[2,5,128,128]{3,2,1,0:T(8,128)S(1)}, f32[2,5,128,128]{3,2,1,0:T(8,128)S(1)}, u32[]{:S(2)}, u32[]{:S(2)}) collective-permute-start(f32[2,5,128,128]{3,2,1,0:T(8,128)S(1)} %get-tuple-element.30), channel_id=1, source_target_pairs={{2,4},{4,2},{6,8},{8,6},{10,12},{12,10},{14,16},{16,14},{18,20},{2... | collective-permute-start | bytes 1966088 | tf_op jit(solution)/shard_map/ppermute | solution.py:531
  55.4 0.0 copy-start.3
  55.4 0.3 collective-permute-start.7
  55.7 2.6 %shard_map.98.after_ref.first_ref = f32[2,8,128,128]{3,2,1,0:T(8,128)S(1)} custom-call(f32[8,8]{1,0:T(8,128)S(1)} %get-tuple-element.21.mix_ref, f32[2,3,128,128]{3,2,1,0:T(8,128)S(1)} %collective-permute-done.5.face_ref, bf16[2,256,256]{2,1,0:T(8,128)(2,1)S(1)} %get-tuple-element.23.z_ref.y_ref.yi_ref, ...), custom_call_target="tpu_custom_call" | custom-call | flops 60000002048 | bytes 60000000 | tf_op jit(solution)/shard_map/pallas_call | solution.py:462
  58.3 0.1 collective-permute-done.7.near_ref
  58.3 5.8 %shard_map.99.hat_ref = f32[2,32,128,128]{3,2,1,0:T(8,128)S(1)} custom-call(f32[4]{0:T(128)S(1)} %add_convert_fusion.side_ref, s32[4]{0:T(128)S(1)} %add_add_fusion.place_ref.after_ref, f32[16,8]{1,0:T(8,128)S(1)} %get-tuple-element.27.mix_x_ref, f32[2,8,8,128]{3,2,1,0:T(8,128)S(1)} %get-tuple-element.25.mix_y_ref, ...), custom_call_target="tpu_custom_call" | custom-call | flops 1000000000 | bytes 1000000 | tf_op jit(solution)/shard_map/pallas_call | solution.py:462
  64.1 5.5 %collective-permute-done.6.face_ref = f32[2,32,8,128]{3,2,1,0:T(8,128)S(1)} collective-permute-done((f32[2,32,8,128]{3,2,1,0:T(8,128)S(1)}, f32[2,32,8,128]{3,2,1,0:T(8,128)S(1)}, u32[]{:S(2)}, u32[]{:S(2)}) %collective-permute-start.6) | collective-permute-done | bytes 262176 | tf_op jit(solution)/shard_map/ppermute | solution.py:528
  69.6 6.8 %shard_map.100.part_ref = f32[2,32,128,128]{3,2,1,0:T(8,128)S(1)} custom-call(f32[4]{0:T(128)S(1)} %add_convert_fusion.side_ref, s32[4]{0:T(128)S(1)} %add_add_fusion.place_ref.after_ref, f32[2,8,8,128]{3,2,1,0:T(8,128)S(1)} %get-tuple-element.25.mix_y_ref, f32[2,32,8,128]{3,2,1,0:T(8,128)S(1)} %collective-permute-done.6.face_ref, ...), custom_call_target="tpu_custom_call" | custom-call | flops 30000001024 | bytes 30000000 | tf_op jit(solution)/shard_map/pallas_call | solution.py:462
  76.4 0.0 collective-permute-done.4.second_ref
  76.4 8.8 %shard_map.101 = f32[2,32,128,128]{3,2,1,0:T(8,128)} custom-call(s32[4]{0:T(128)S(1)} %add_add_fusion.place_ref.after_ref, f32[8,8]{1,0:T(8,128)S(1)} %get-tuple-element.21.mix_ref, f32[2,5,128,128]{3,2,1,0:T(8,128)S(1)} %collective-permute-done.4.second_ref, f32[2,8,128,128]{3,2,1,0:T(8,128)S(1)} %shard_map.98.after_ref.first_ref, ...), custom_call_target="tpu_custom_call" | custom-call | flops 1000000000 | bytes 1000000 | tf_op jit(solution)/shard_map/pallas_call | solution.py:560
  (17 shorter events, 0.0 us)
Async XLA Ops:
  0.0 11.6 %copy-start.6 = (f32[256,256]{1,0:T(8,128)S(1)}, f32[256,256]{1,0:T(8,128)}, u32[]{:S(2)}) copy-start(f32[256,256]{1,0:T(8,128)} %constant.35.clone.inverse_ref) | copy-start | bytes 786436
  0.0 11.6 %copy-start.7 = (f32[256,256]{1,0:T(8,128)S(1)}, f32[256,256]{1,0:T(8,128)}, u32[]{:S(2)}) copy-start(f32[256,256]{1,0:T(8,128)} %constant.34.clone.forward_ref) | copy-start | bytes 786436
  0.0 11.6 %copy-start.9 = (f32[8,8]{1,0:T(8,128)S(1)}, f32[8,8]{1,0:T(8,128)}, u32[]{:S(2)}) copy-start(f32[8,8]{1,0:T(8,128)} %y_coupling_ref.1) | copy-start | bytes 772
  0.0 11.6 %copy-start.8 = (f32[8,8]{1,0:T(8,128)S(1)}, f32[8,8]{1,0:T(8,128)}, u32[]{:S(2)}) copy-start(f32[8,8]{1,0:T(8,128)} %x_ref.1) | copy-start | bytes 772
  0.1 18.1 %copy-start = (f32[2,32,128,128]{3,2,1,0:T(8,128)S(1)}, f32[2,32,128,128]{3,2,1,0:T(8,128)}, u32[]{:S(2)}) copy-start(f32[2,32,128,128]{3,2,1,0:T(8,128)} %field_ref.9) | copy-start | bytes 12582916
  0.1 18.1 %copy-start.1 = (f32[32,128,128]{2,1,0:T(8,128)S(1)}, f32[32,128,128]{2,1,0:T(8,128)}, u32[]{:S(2)}) copy-start(f32[32,128,128]{2,1,0:T(8,128)} %wave_ref.9) | copy-start | bytes 6291460
  2.5 15.8 %collective-permute-start.3 = (f32[2,8,128,128]{3,2,1,0:T(8,128)S(1)}, f32[2,8,128,128]{3,2,1,0:T(8,128)S(1)}, u32[]{:S(2)}, u32[]{:S(2)}) collective-permute-start(f32[2,8,128,128]{3,2,1,0:T(8,128)S(1)} %get-tuple-element.28), channel_id=1, source_target_pairs={{0,2},{2,0},{4,6},{6,4},{8,10},{10,8},{12,14},{14,12},{16,18},{18,... | collective-permute-start | bytes 3145736 | tf_op jit(solution)/shard_map/ppermute | solution.py:530
  2.6 23.7 %collective-permute-start.2 = (f32[2,32,8,128]{3,2,1,0:T(8,128)S(1)}, f32[2,32,8,128]{3,2,1,0:T(8,128)S(1)}, u32[]{:S(2)}, u32[]{:S(2)}) collective-permute-start(f32[2,32,8,128]{3,2,1,0:T(8,128)S(1)} %get-tuple-element.26), channel_id=1, source_target_pairs={{0,1},{1,0},{2,3},{3,2},{4,5},{5,4},{6,7},{7,6},{8,9},{9,8},{10,11... | collective-permute-start | bytes 786440 | tf_op jit(solution)/shard_map/ppermute | solution.py:528
  6.5 26.6 %collective-permute-start.1 = (f32[2,3,128,128]{3,2,1,0:T(8,128)S(1)}, f32[2,3,128,128]{3,2,1,0:T(8,128)S(1)}, u32[]{:S(2)}, u32[]{:S(2)}) collective-permute-start(f32[2,3,128,128]{3,2,1,0:T(8,128)S(1)} %get-tuple-element.20.after_ref), channel_id=1, source_target_pairs={{2,4},{4,2},{6,8},{8,6},{10,12},{12,10},{14,16},{16,14},{18,20},{2... | collective-permute-start | bytes 1179656 | tf_op jit(solution)/shard_map/ppermute | solution.py:529
  14.7 21.0 %collective-permute-start = (f32[2,5,128,128]{3,2,1,0:T(8,128)S(1)}, f32[2,5,128,128]{3,2,1,0:T(8,128)S(1)}, u32[]{:S(2)}, u32[]{:S(2)}) collective-permute-start(f32[2,5,128,128]{3,2,1,0:T(8,128)S(1)} %get-tuple-element.22), channel_id=1, source_target_pairs={{2,4},{4,2},{6,8},{8,6},{10,12},{12,10},{14,16},{16,14},{18,20},{2... | collective-permute-start | bytes 1966088 | tf_op jit(solution)/shard_map/ppermute | solution.py:531
  18.3 2.2 %copy-start.2 = (f32[2,32,128,128]{3,2,1,0:T(8,128)S(1)}, f32[2,32,128,128]{3,2,1,0:T(8,128)}, u32[]{:S(2)}) copy-start(f32[2,32,128,128]{3,2,1,0:T(8,128)} %source_ref.3) | copy-start | bytes 12582916
  20.5 5.8 %copy-start.4 = (f32[17,2,128,128]{3,2,1,0:T(8,128)S(1)}, f32[17,2,128,128]{3,2,1,0:T(8,128)}, u32[]{:S(2)}) copy-start(f32[17,2,128,128]{3,2,1,0:T(8,128)} %constant.36.clone.green_ref) | copy-start | bytes 6684676
  33.1 2.6 %copy-start.5 = (f32[8,2,128,128]{3,2,1,0:T(8,128)S(1)}, f32[8,2,128,128]{3,2,1,0:T(8,128)}, u32[]{:S(2)}) copy-start(f32[8,2,128,128]{3,2,1,0:T(8,128)} %constant.37.clone.line_ref) | copy-start | bytes 3145732
  38.1 17.6 %collective-permute-start.5 = (f32[2,3,128,128]{3,2,1,0:T(8,128)S(1)}, f32[2,3,128,128]{3,2,1,0:T(8,128)S(1)}, u32[]{:S(2)}, u32[]{:S(2)}) collective-permute-start(f32[2,3,128,128]{3,2,1,0:T(8,128)S(1)} %get-tuple-element.31), channel_id=1, source_target_pairs={{2,4},{4,2},{6,8},{8,6},{10,12},{12,10},{14,16},{16,14},{18,20},{2... | collective-permute-start | bytes 1179656 | tf_op jit(solution)/shard_map/ppermute | solution.py:529
  51.8 17.8 %collective-permute-start.6 = (f32[2,32,8,128]{3,2,1,0:T(8,128)S(1)}, f32[2,32,8,128]{3,2,1,0:T(8,128)S(1)}, u32[]{:S(2)}, u32[]{:S(2)}) collective-permute-start(f32[2,32,8,128]{3,2,1,0:T(8,128)S(1)} %get-tuple-element.32), channel_id=1, source_target_pairs={{0,1},{1,0},{2,3},{3,2},{4,5},{5,4},{6,7},{7,6},{8,9},{9,8},{10,11... | collective-permute-start | bytes 786440 | tf_op jit(solution)/shard_map/ppermute | solution.py:528
  53.0 23.4 %collective-permute-start.4 = (f32[2,5,128,128]{3,2,1,0:T(8,128)S(1)}, f32[2,5,128,128]{3,2,1,0:T(8,128)S(1)}, u32[]{:S(2)}, u32[]{:S(2)}) collective-permute-start(f32[2,5,128,128]{3,2,1,0:T(8,128)S(1)} %get-tuple-element.30), channel_id=1, source_target_pairs={{2,4},{4,2},{6,8},{8,6},{10,12},{12,10},{14,16},{16,14},{18,20},{2... | collective-permute-start | bytes 1966088 | tf_op jit(solution)/shard_map/ppermute | solution.py:531
  55.4 2.9 %copy-start.3 = (f32[2,32,128,128]{3,2,1,0:T(8,128)S(1)}, f32[2,32,128,128]{3,2,1,0:T(8,128)}, u32[]{:S(2)}) copy-start(f32[2,32,128,128]{3,2,1,0:T(8,128)} %source_ref.3) | copy-start | bytes 12582916
  55.4 2.9 %collective-permute-start.7 = (f32[2,8,128,128]{3,2,1,0:T(8,128)S(1)}, f32[2,8,128,128]{3,2,1,0:T(8,128)S(1)}, u32[]{:S(2)}, u32[]{:S(2)}) collective-permute-start(f32[2,8,128,128]{3,2,1,0:T(8,128)S(1)} %get-tuple-element.34), channel_id=1, source_target_pairs={{0,2},{2,0},{4,6},{6,4},{8,10},{10,8},{12,14},{14,12},{16,18},{18,... | collective-permute-start | bytes 3145736 | tf_op jit(solution)/shard_map/ppermute | solution.py:530

commit v4 on v3

--- a/solution.py
+++ b/solution.py
@@ -305,6 +305,65 @@
             out_ref[1, x, rows, :] = im
 
 
+def lines_kernel(hat_ref, y_ref, out_ref):
+    group = 16
+
+    @pl.loop(0, CX // group)
+    def _(i):
+        planes = [(hat_ref[0, i * group + k], hat_ref[1, i * group + k]) for k in range(group)]
+        for k, (re, im) in enumerate(y_product(planes, y_ref)):
+            out_ref[0, i * group + k] = re
+            out_ref[1, i * group + k] = im
+
+    @tiles(N, 8)
+    def _(rows):
+        given = [(out_ref[0, x, rows, :], out_ref[1, x, rows, :]) for x in range(CX)]
+        for x, (re, im) in enumerate(fft(given, -1)):
+            out_ref[0, x, rows, :] = re
+            out_ref[1, x, rows, :] = im
+
+
+def late_side_kernel(
+    side_ref, place_ref, mix_y_ref, face_ref, part_ref, z_ref, y_ref, out_ref, rows_ref, wide_ref
+):
+    mix_ref = mix_y_ref.at[place_ref[3]]
+
+    @pl.loop(0, CX)
+    def _(x):
+        for part in range(2):
+            tile = face_ref[part, lax.rem(x + place_ref[0], CX)]
+            total = mix_ref[0] * tile[0:1]
+            for b in range(1, RIM):
+                total += mix_ref[b] * tile[b : b + 1]
+            rows_ref[pl.ds(pl.multiple_of(x * RIM, RIM), RIM), part * N : (part + 1) * N] = -total
+
+    wide_ref[...] = from_right(rows_ref[...], z_ref)
+    spans = [slice(x * RIM, (x + 1) * RIM) for x in range(CX)]
+    spectrum = fft([(wide_ref[span, :N], wide_ref[span, N:]) for span in spans], -1)
+    for span, (re, im) in zip(spans, spectrum):
+        wide_ref[span, :N] = re
+        wide_ref[span, N:] = im
+    low, high = side_ref[2], side_ref[3]
+    middle = jnp.zeros((N - 2 * RIM, N), F32)
+    group = 16
+
+    @pl.loop(0, CX // group)
+    def _(i):
+        terms = wide_ref[pl.ds(pl.multiple_of(i * group * RIM, group * RIM), group * RIM), :]
+        planes = []
+        for k in range(group):
+            term = terms[k * RIM : (k + 1) * RIM]
+            planes.append(
+                tuple(
+                    jnp.concatenate([low * value, middle, high * value], axis=0)
+                    for value in (term[:, :N], term[:, N:])
+                )
+            )
+        for k, (re, im) in enumerate(y_product(planes, y_ref)):
+            out_ref[0, i * group + k] = part_ref[0, i * group + k] + re
+            out_ref[1, i * group + k] = part_ref[1, i * group + k] + im
+
+
 def first_kernel(mix_ref, face_ref, z_ref, y_ref, after_ref, out_ref):
     @tiles(N, 16)
     def _(rows):
@@ -356,7 +415,7 @@
         out_ref[1, k] = im
 
 
-def filter_far(given_of, part_ref, green_ref, z_ref, ring_refs, work_ref):
+def filter_far(given_of, part_ref, green_ref, z_ref, ring_refs, work_ref, filtered_part=True):
     ring = len(ring_refs)
 
     @pl.loop(0, N // (8 * ring))
@@ -364,9 +423,12 @@
         for j, ring_ref in enumerate(ring_refs):
             rows = pl.ds(pl.multiple_of(i * 8 * ring, 8 * ring) + 8 * j, 8)
             spectrum = fft_of_first(given_of(rows), CX)
+            local = [(part_ref[0, x, rows, :], part_ref[1, x, rows, :]) for x in range(CX)]
+            if not filtered_part:
+                spectrum = [(a + c, b + d) for (a, b), (c, d) in zip(spectrum, local)]
             for x, (re, im) in enumerate(filtered(spectrum, green_ref, rows)):
-                ring_ref[0, x] = part_ref[0, x, rows, :] + re
-                ring_ref[1, x] = part_ref[1, x, rows, :] + im
+                ring_ref[0, x] = local[x][0] + re if filtered_part else re
+                ring_ref[1, x] = local[x][1] + im if filtered_part else im
             planes = [(ring_ref[0, x], ring_ref[1, x]) for x in range(CX)]
             for x, (re, im) in enumerate(z_product(planes, z_ref)):
                 work_ref[0, x, rows, :] = re
@@ -419,7 +481,7 @@
         return list(zip(*sums))
 
     base = place_ref[0]
-    filter_far(given_of, part_ref, green_ref, zi_ref, ring_refs, work_ref)
+    filter_far(given_of, part_ref, green_ref, zi_ref, ring_refs, work_ref, filtered_part=False)
     copies = []
     for first in range(0, CX, RIM):
         step_back(base, first, RIM, work_ref, field_ref, wave_ref, yi_ref, done_ref)
@@ -541,10 +603,17 @@
             local_kernel, (weights, place, mix_x), (mix_y, field, source, wave, near_in, zf), VOLUME,
             after=place if first is None else first,
         )
-        part = call(
-            side_kernel, (weights, place), (mix_y, side_in, hat, zf, yf, green), VOLUME, (rows, rows),
-            weight=30,
-        )
+        if step == 0:
+            part = call(
+                side_kernel, (weights, place), (mix_y, side_in, hat, zf, yf, green), VOLUME, (rows, rows),
+                weight=30,
+            )
+        else:
+            lines_in = call(lines_kernel, (), (hat, yf), VOLUME)
+            part = call(
+                late_side_kernel, (weights, place), (mix_y, side_in, lines_in, zf, yf), VOLUME, (rows, rows),
+                weight=30,
+            )
         if first is None:
             first = far_part(part)
         if step == 0:

time: 85.6 us -> 82.8 us (0.967)
  waiting for transfers between devices: 5.54 us -> 1.82 us
  Pallas kernels: 55.5 us -> 56.4 us
    ppermute x2, waiting for transfers between devices: 5.47 us -> 1.75 us  [body(): side_in = lax.ppermute(side_out, 'gy', side_pairs)]
    pallas_call x8 -> x9, Pallas kernels: 41.3 us -> 41.7 us  [call(): pl.pallas_call(kernel, in_specs=[SMEM] * len(scalars) + [WHOLE] * len(ope...]
    unnamed x20 -> x24, local copies, waits for them, and re-layouts: 2.22 us -> 2.24 us
  transfers between devices with their start and end apart: 8 -> 8, of which waited for: 2 -> 2; matrix products, arithmetic and copies ran while one was open for 0% -> 0% of each run, Pallas kernels for 49% -> 51%
where the time goes in v4:
time: 82.8 us; the launch traced here: 82.6 us
  Pallas kernels  56.4 us (68%)
  starting transfers between devices  21.5 us (26%)
  local copies, waits for them, and re-layouts  2.24 us (3%)
  waiting for transfers between devices  1.82 us (2%)
    pallas_call x9, Pallas kernels, call(): pl.pallas_call(kernel, in_specs=[SMEM] * len(scalars) + [WHOLE] * len(ope...  41.7 us
    ppermute x2, starting transfers between devices, body(): first_in = lax.ppermute(first_out, 'gx', far_pairs)  10.1 us
    pallas_call x1, Pallas kernels, body(): pl.pallas_call(last_kernel, in_specs=[SMEM] * 2 + [WHOLE] * 8, out_specs=...  9.28 us
    ppermute x2, starting transfers between devices, body(): second_in = lax.ppermute(second_out, 'gx', far_pairs)  5.89 us
    ppermute x2, starting transfers between devices, body(): side_in = lax.ppermute(side_out, 'gy', side_pairs)  5.19 us
    pallas_call x1, Pallas kernels, prepare(): pl.pallas_call(spectrum_kernel, in_specs=[SMEM] * 3 + [HBM] + [WHOLE] * 2...  3.05 us
    pallas_call x1, Pallas kernels, cut_faces(): pl.pallas_call(cut_kernel, in_specs=[SMEM, HBM], out_specs=(WHOLE,) * 3,...  2.33 us
    unnamed x24, local copies, waits for them, and re-layouts  2.24 us
  transfers between devices with their start and end apart: 8, of which 2 were waited for; matrix products, arithmetic and copies ran while one was open for 0% of the time, Pallas kernels for 51%

profile of v4, /device:TPU:24, one launch (start us, length us, event | category | flops | bytes accessed | tf_op | source)
XLA Modules:
  0.0 82.6 jit_solution(7168167413867428257)
XLA Ops:
  0.0 0.1 add_add_fusion.place_ref.after_ref
  0.1 2.3 %shard_map.91 = (f32[2,32,8,128]{3,2,1,0:T(8,128)S(1)}, f32[2,3,128,128]{3,2,1,0:T(8,128)S(1)}, f32[2,8,128,128]{3,2,1,0:T(8,128)S(1)}) custom-call(s32[4]{0:T(128)S(1)} %add_add_fusion.place_ref.after_ref, f32[2,32,128,128]{3,2,1,0:T(8,128)} %field_ref.9), custom_call_target="tpu_custom_call" | custom-call | flops 1000000000 | bytes 1000000 | tf_op jit(solution)/shard_map/pallas_call | solution.py:555
  2.5 0.1 collective-permute-start.3
  2.6 4.0 %collective-permute-start.2 = (f32[2,32,8,128]{3,2,1,0:T(8,128)S(1)}, f32[2,32,8,128]{3,2,1,0:T(8,128)S(1)}, u32[]{:S(2)}, u32[]{:S(2)}) collective-permute-start(f32[2,32,8,128]{3,2,1,0:T(8,128)S(1)} %get-tuple-element.26), channel_id=1, source_target_pairs={{0,1},{1,0},{2,3},{3,2},{4,5},{5,4},{6,7},{7,6},{8,9},{9,8},{10,11... | collective-permute-start | bytes 786440 | tf_op jit(solution)/shard_map/ppermute | solution.py:590
  6.5 5.0 %collective-permute-start.1 = (f32[2,3,128,128]{3,2,1,0:T(8,128)S(1)}, f32[2,3,128,128]{3,2,1,0:T(8,128)S(1)}, u32[]{:S(2)}, u32[]{:S(2)}) collective-permute-start(f32[2,3,128,128]{3,2,1,0:T(8,128)S(1)} %get-tuple-element.20.after_ref), channel_id=1, source_target_pairs={{2,4},{4,2},{6,8},{8,6},{10,12},{12,10},{14,16},{16,14},{18,20},{2... | collective-permute-start | bytes 1179656 | tf_op jit(solution)/shard_map/ppermute | solution.py:591
  11.6 3.0 %shard_map.92 = (f32[16,8]{1,0:T(8,128)S(1)}, f32[8,8]{1,0:T(8,128)S(1)}, f32[2,8,8,128]{3,2,1,0:T(8,128)S(1)}, f32[2,5,128,128]{3,2,1,0:T(8,128)S(1)}, bf16[2,2...) custom-call(s32[4]{0:T(128)S(1)} %add_add_fusion.place_ref.after_ref, f32[8,8]{1,0:T(8,128)S(1)} %copy-done.10, ...), custom_call_target="tpu_custom_call" | custom-call | flops 1000000000 | bytes 1000000 | tf_op jit(solution)/shard_map/pallas_call | solution.py:541
  14.7 0.0 copy-start.8
  14.7 3.5 %collective-permute-start = (f32[2,5,128,128]{3,2,1,0:T(8,128)S(1)}, f32[2,5,128,128]{3,2,1,0:T(8,128)S(1)}, u32[]{:S(2)}, u32[]{:S(2)}) collective-permute-start(f32[2,5,128,128]{3,2,1,0:T(8,128)S(1)} %get-tuple-element.22), channel_id=1, source_target_pairs={{2,4},{4,2},{6,8},{8,6},{10,12},{12,10},{14,16},{16,14},{18,20},{2... | collective-permute-start | bytes 1966088 | tf_op jit(solution)/shard_map/ppermute | solution.py:593
  18.2 0.1 add_convert_fusion.side_ref
  18.3 0.0 collective-permute-done.3.near_ref
  18.3 0.0 copy-start.2
  18.3 2.2 %copy-done.2 = f32[2,32,128,128]{3,2,1,0:T(8,128)S(1)} copy-done((f32[2,32,128,128]{3,2,1,0:T(8,128)S(1)}, f32[2,32,128,128]{3,2,1,0:T(8,128)}, u32[]{:S(2)}) %copy-start.2) | copy-done | bytes 4194328
  20.5 5.8 %shard_map.93.hat_ref = f32[2,32,128,128]{3,2,1,0:T(8,128)S(1)} custom-call(f32[4]{0:T(128)S(1)} %add_convert_fusion.side_ref, s32[4]{0:T(128)S(1)} %add_add_fusion.place_ref.after_ref, f32[16,8]{1,0:T(8,128)S(1)} %get-tuple-element.27.mix_x_ref, f32[2,8,8,128]{3,2,1,0:T(8,128)S(1)} %get-tuple-element.25.mix_y_ref, f32[2,32,128,128]{3,2,1,0:T(8,128)S(1)} %copy-done, ...), custom_call_target="tpu_custom_call" | custom-call | flops 1000000000 | bytes 1000000 | tf_op jit(solution)/shard_map/pallas_call | solution.py:524
  26.3 0.0 collective-permute-done.2.face_ref
  26.3 6.8 %shard_map.94.after_ref.part_ref = f32[2,32,128,128]{3,2,1,0:T(8,128)S(1)} custom-call(f32[4]{0:T(128)S(1)} %add_convert_fusion.side_ref, s32[4]{0:T(128)S(1)} %add_add_fusion.place_ref.after_ref, f32[2,8,8,128]{3,2,1,0:T(8,128)S(1)} %get-tuple-element.25.mix_y_ref, f32[2,32,8,128]{3,2,1,0:T(8,128)S(1)} %collective-permute-done.2.face_ref, ...), custom_call_target="tpu_custom_call" | custom-call | flops 30000001024 | bytes 30000000 | tf_op jit(solution)/shard_map/pallas_call | solution.py:524
  33.1 0.0 copy-start.5
  33.1 2.6 %shard_map.95.first_ref = f32[2,8,128,128]{3,2,1,0:T(8,128)S(1)} custom-call(f32[8,8]{1,0:T(8,128)S(1)} %get-tuple-element.21.mix_ref, f32[2,3,128,128]{3,2,1,0:T(8,128)S(1)} %collective-permute-done.1.face_ref, bf16[2,256,256]{2,1,0:T(8,128)(2,1)S(1)} %get-tuple-element.23.z_ref.y_ref.yi_ref, bf16[2,256,256]{2,1,0:T(8,128)(2,1)S(1)} %get-tuple-element.24.y_ref.z_ref.zi_ref, ...), custom_call_target="tpu_custom_call" | custom-call | flops 60000002048 | bytes 60000000 | tf_op jit(solution)/shard_map/pallas_call | solution.py:524
  35.7 2.3 %shard_map.96 = (f32[2,8,128,128]{3,2,1,0:T(8,128)S(1)}, f32[2,3,128,128]{3,2,1,0:T(8,128)S(1)}) custom-call(s32[4]{0:T(128)S(1)} %add_add_fusion.place_ref.after_ref, f32[8,8]{1,0:T(8,128)S(1)} %get-tuple-element.21.mix_ref, f32[2,5,128,128]{3,2,1,0:T(8,128)S(1)} %collective-permute-done.second_ref, f32[2,8,128,128]{3,2,1,0:T(8,128)S(1)} %shard_map.95.first_ref, ...), custom_call_target="tpu_custom_call" | custom-call | flops 1000000000 | bytes 1000000 | tf_op jit(solution)/shard_map/pallas_call | solution.py:524
  38.1 5.1 %collective-permute-start.5 = (f32[2,3,128,128]{3,2,1,0:T(8,128)S(1)}, f32[2,3,128,128]{3,2,1,0:T(8,128)S(1)}, u32[]{:S(2)}, u32[]{:S(2)}) collective-permute-start(f32[2,3,128,128]{3,2,1,0:T(8,128)S(1)} %get-tuple-element.31), channel_id=1, source_target_pairs={{2,4},{4,2},{6,8},{8,6},{10,12},{12,10},{14,16},{16,14},{18,20},{2... | collective-permute-start | bytes 1179656 | tf_op jit(solution)/shard_map/ppermute | solution.py:591
  43.1 8.6 %shard_map.97 = (f32[2,32,128,128]{3,2,1,0:T(8,128)S(1)}, f32[2,32,8,128]{3,2,1,0:T(8,128)S(1)}, f32[2,8,128,128]{3,2,1,0:T(8,128)S(1)}, f32[2,5,128,128]{3,2,1,0:T(8,128)S(1)}) custom-call(s32[4]{0:T(128)S(1)} %add_add_fusion.place_ref.after_ref, f32[2,8,128,128]{3,2,1,0:T(8,128)S(1)} %get-tuple-element.29.hat_ref, ...), custom_call_target="tpu_custom_call" | custom-call | flops 1000000000 | bytes 1000000 | tf_op jit(solution)/shard_map/pallas_call | solution.py:524
  51.8 1.2 %collective-permute-start.6 = (f32[2,32,8,128]{3,2,1,0:T(8,128)S(1)}, f32[2,32,8,128]{3,2,1,0:T(8,128)S(1)}, u32[]{:S(2)}, u32[]{:S(2)}) collective-permute-start(f32[2,32,8,128]{3,2,1,0:T(8,128)S(1)} %get-tuple-element.32), channel_id=1, source_target_pairs={{0,1},{1,0},{2,3},{3,2},{4,5},{5,4},{6,7},{7,6},{8,9},{9,8},{10,11... | collective-permute-start | bytes 786440 | tf_op jit(solution)/shard_map/ppermute | solution.py:590
  53.0 2.4 %collective-permute-start.4 = (f32[2,5,128,128]{3,2,1,0:T(8,128)S(1)}, f32[2,5,128,128]{3,2,1,0:T(8,128)S(1)}, u32[]{:S(2)}, u32[]{:S(2)}) collective-permute-start(f32[2,5,128,128]{3,2,1,0:T(8,128)S(1)} %get-tuple-element.30), channel_id=1, source_target_pairs={{2,4},{4,2},{6,8},{8,6},{10,12},{12,10},{14,16},{16,14},{18,20},{2... | collective-permute-start | bytes 1966088 | tf_op jit(solution)/shard_map/ppermute | solution.py:593
  55.4 0.0 copy-start.3
  55.4 0.0 copy-start.9
  55.4 0.3 collective-permute-start.7
  55.7 2.6 %shard_map.98.after_ref.first_ref = f32[2,8,128,128]{3,2,1,0:T(8,128)S(1)} custom-call(f32[8,8]{1,0:T(8,128)S(1)} %get-tuple-element.21.mix_ref, f32[2,3,128,128]{3,2,1,0:T(8,128)S(1)} %collective-permute-done.5.face_ref, bf16[2,256,256]{2,1,0:T(8,128)(2,1)S(1)} %get-tuple-element.23.z_ref.y_ref.yi_ref, ...), custom_call_target="tpu_custom_call" | custom-call | flops 60000002048 | bytes 60000000 | tf_op jit(solution)/shard_map/pallas_call | solution.py:524
  58.3 0.1 collective-permute-done.7.near_ref
  58.4 5.8 %shard_map.99.hat_ref = f32[2,32,128,128]{3,2,1,0:T(8,128)S(1)} custom-call(f32[4]{0:T(128)S(1)} %add_convert_fusion.side_ref, s32[4]{0:T(128)S(1)} %add_add_fusion.place_ref.after_ref, f32[16,8]{1,0:T(8,128)S(1)} %copy-done.9, f32[2,8,8,128]{3,2,1,0:T(8,128)S(1)} %get-tuple-element.25.mix_y_ref, f32[2,32,128,128]{3,2,1,0:T(8,128)S(1)} %get-tuple-element.33.field_ref, ...), custom_call_target="tpu_custom_call" | custom-call | flops 1000000000 | bytes 1000000 | tf_op jit(solution)/shard_map/pallas_call | solution.py:524
  64.1 3.8 %shard_map.100.part_ref = f32[2,32,128,128]{3,2,1,0:T(8,128)S(1)} custom-call(f32[2,32,128,128]{3,2,1,0:T(8,128)S(1)} %shard_map.99.hat_ref, bf16[2,256,256]{2,1,0:T(8,128)(2,1)S(1)} %get-tuple-element.24.y_ref.z_ref.zi_ref), custom_call_target="tpu_custom_call" | custom-call | flops 1000000000 | bytes 1000000 | tf_op jit(solution)/shard_map/pallas_call | solution.py:524
  67.9 1.7 %collective-permute-done.6.face_ref = f32[2,32,8,128]{3,2,1,0:T(8,128)S(1)} collective-permute-done((f32[2,32,8,128]{3,2,1,0:T(8,128)S(1)}, f32[2,32,8,128]{3,2,1,0:T(8,128)S(1)}, u32[]{:S(2)}, u32[]{:S(2)}) %collective-permute-start.6) | collective-permute-done | bytes 262176 | tf_op jit(solution)/shard_map/ppermute | solution.py:590
  69.6 3.5 %shard_map.101.part_ref = f32[2,32,128,128]{3,2,1,0:T(8,128)S(1)} custom-call(f32[4]{0:T(128)S(1)} %add_convert_fusion.side_ref, s32[4]{0:T(128)S(1)} %add_add_fusion.place_ref.after_ref, f32[2,8,8,128]{3,2,1,0:T(8,128)S(1)} %get-tuple-element.25.mix_y_ref, f32[2,32,8,128]{3,2,1,0:T(8,128)S(1)} %collective-permute-done.6.face_ref, ...), custom_call_target="tpu_custom_call" | custom-call | flops 30000001024 | bytes 30000000 | tf_op jit(solution)/shard_map/pallas_call | solution.py:524
  73.1 9.3 %shard_map.102 = f32[2,32,128,128]{3,2,1,0:T(8,128)} custom-call(s32[4]{0:T(128)S(1)} %add_add_fusion.place_ref.after_ref, f32[8,8]{1,0:T(8,128)S(1)} %get-tuple-element.21.mix_ref, f32[2,5,128,128]{3,2,1,0:T(8,128)S(1)} %collective-permute-done.4.second_ref, f32[2,8,128,128]{3,2,1,0:T(8,128)S(1)} %shard_map.98.after_ref.first_ref, ...), custom_call_target="tpu_custom_call" | custom-call | flops 1000000000 | bytes 1000000 | tf_op jit(solution)/shard_map/pallas_call | solution.py:629
  (22 shorter events, 0.0 us)
Async XLA Ops:
  0.0 11.6 %copy-start.6 = (f32[256,256]{1,0:T(8,128)S(1)}, f32[256,256]{1,0:T(8,128)}, u32[]{:S(2)}) copy-start(f32[256,256]{1,0:T(8,128)} %constant.35.clone.inverse_ref) | copy-start | bytes 786436
  0.0 11.6 %copy-start.7 = (f32[256,256]{1,0:T(8,128)S(1)}, f32[256,256]{1,0:T(8,128)}, u32[]{:S(2)}) copy-start(f32[256,256]{1,0:T(8,128)} %constant.34.clone.forward_ref) | copy-start | bytes 786436
  0.0 11.6 %copy-start.11 = (f32[8,8]{1,0:T(8,128)S(1)}, f32[8,8]{1,0:T(8,128)}, u32[]{:S(2)}) copy-start(f32[8,8]{1,0:T(8,128)} %y_coupling_ref.1) | copy-start | bytes 772
  0.0 11.6 %copy-start.10 = (f32[8,8]{1,0:T(8,128)S(1)}, f32[8,8]{1,0:T(8,128)}, u32[]{:S(2)}) copy-start(f32[8,8]{1,0:T(8,128)} %x_ref.1) | copy-start | bytes 772
  0.1 18.2 %copy-start = (f32[2,32,128,128]{3,2,1,0:T(8,128)S(1)}, f32[2,32,128,128]{3,2,1,0:T(8,128)}, u32[]{:S(2)}) copy-start(f32[2,32,128,128]{3,2,1,0:T(8,128)} %field_ref.9) | copy-start | bytes 12582916
  0.1 18.2 %copy-start.1 = (f32[32,128,128]{2,1,0:T(8,128)S(1)}, f32[32,128,128]{2,1,0:T(8,128)}, u32[]{:S(2)}) copy-start(f32[32,128,128]{2,1,0:T(8,128)} %wave_ref.9) | copy-start | bytes 6291460
  2.5 15.8 %collective-permute-start.3 = (f32[2,8,128,128]{3,2,1,0:T(8,128)S(1)}, f32[2,8,128,128]{3,2,1,0:T(8,128)S(1)}, u32[]{:S(2)}, u32[]{:S(2)}) collective-permute-start(f32[2,8,128,128]{3,2,1,0:T(8,128)S(1)} %get-tuple-element.28), channel_id=1, source_target_pairs={{0,2},{2,0},{4,6},{6,4},{8,10},{10,8},{12,14},{14,12},{16,18},{18,... | collective-permute-start | bytes 3145736 | tf_op jit(solution)/shard_map/ppermute | solution.py:592
  2.6 23.7 %collective-permute-start.2 = (f32[2,32,8,128]{3,2,1,0:T(8,128)S(1)}, f32[2,32,8,128]{3,2,1,0:T(8,128)S(1)}, u32[]{:S(2)}, u32[]{:S(2)}) collective-permute-start(f32[2,32,8,128]{3,2,1,0:T(8,128)S(1)} %get-tuple-element.26), channel_id=1, source_target_pairs={{0,1},{1,0},{2,3},{3,2},{4,5},{5,4},{6,7},{7,6},{8,9},{9,8},{10,11... | collective-permute-start | bytes 786440 | tf_op jit(solution)/shard_map/ppermute | solution.py:590
  6.5 26.6 %collective-permute-start.1 = (f32[2,3,128,128]{3,2,1,0:T(8,128)S(1)}, f32[2,3,128,128]{3,2,1,0:T(8,128)S(1)}, u32[]{:S(2)}, u32[]{:S(2)}) collective-permute-start(f32[2,3,128,128]{3,2,1,0:T(8,128)S(1)} %get-tuple-element.20.after_ref), channel_id=1, source_target_pairs={{2,4},{4,2},{6,8},{8,6},{10,12},{12,10},{14,16},{16,14},{18,20},{2... | collective-permute-start | bytes 1179656 | tf_op jit(solution)/shard_map/ppermute | solution.py:591
  14.7 11.6 %copy-start.8 = (f32[16,8]{1,0:T(8,128)}, f32[16,8]{1,0:T(8,128)S(1)}, u32[]{:S(2)}) copy-start(f32[16,8]{1,0:T(8,128)S(1)} %get-tuple-element.27.mix_x_ref) | copy-start | bytes 1540
  14.7 21.0 %collective-permute-start = (f32[2,5,128,128]{3,2,1,0:T(8,128)S(1)}, f32[2,5,128,128]{3,2,1,0:T(8,128)S(1)}, u32[]{:S(2)}, u32[]{:S(2)}) collective-permute-start(f32[2,5,128,128]{3,2,1,0:T(8,128)S(1)} %get-tuple-element.22), channel_id=1, source_target_pairs={{2,4},{4,2},{6,8},{8,6},{10,12},{12,10},{14,16},{16,14},{18,20},{2... | collective-permute-start | bytes 1966088 | tf_op jit(solution)/shard_map/ppermute | solution.py:593
  18.3 2.2 %copy-start.2 = (f32[2,32,128,128]{3,2,1,0:T(8,128)S(1)}, f32[2,32,128,128]{3,2,1,0:T(8,128)}, u32[]{:S(2)}) copy-start(f32[2,32,128,128]{3,2,1,0:T(8,128)} %source_ref.3) | copy-start | bytes 12582916
  20.5 5.8 %copy-start.4 = (f32[17,2,128,128]{3,2,1,0:T(8,128)S(1)}, f32[17,2,128,128]{3,2,1,0:T(8,128)}, u32[]{:S(2)}) copy-start(f32[17,2,128,128]{3,2,1,0:T(8,128)} %constant.36.clone.green_ref) | copy-start | bytes 6684676
  33.1 2.6 %copy-start.5 = (f32[8,2,128,128]{3,2,1,0:T(8,128)S(1)}, f32[8,2,128,128]{3,2,1,0:T(8,128)}, u32[]{:S(2)}) copy-start(f32[8,2,128,128]{3,2,1,0:T(8,128)} %constant.37.clone.line_ref) | copy-start | bytes 3145732
  38.1 17.6 %collective-permute-start.5 = (f32[2,3,128,128]{3,2,1,0:T(8,128)S(1)}, f32[2,3,128,128]{3,2,1,0:T(8,128)S(1)}, u32[]{:S(2)}, u32[]{:S(2)}) collective-permute-start(f32[2,3,128,128]{3,2,1,0:T(8,128)S(1)} %get-tuple-element.31), channel_id=1, source_target_pairs={{2,4},{4,2},{6,8},{8,6},{10,12},{12,10},{14,16},{16,14},{18,20},{2... | collective-permute-start | bytes 1179656 | tf_op jit(solution)/shard_map/ppermute | solution.py:591
  51.8 17.9 %collective-permute-start.6 = (f32[2,32,8,128]{3,2,1,0:T(8,128)S(1)}, f32[2,32,8,128]{3,2,1,0:T(8,128)S(1)}, u32[]{:S(2)}, u32[]{:S(2)}) collective-permute-start(f32[2,32,8,128]{3,2,1,0:T(8,128)S(1)} %get-tuple-element.32), channel_id=1, source_target_pairs={{0,1},{1,0},{2,3},{3,2},{4,5},{5,4},{6,7},{7,6},{8,9},{9,8},{10,11... | collective-permute-start | bytes 786440 | tf_op jit(solution)/shard_map/ppermute | solution.py:590
  53.0 20.1 %collective-permute-start.4 = (f32[2,5,128,128]{3,2,1,0:T(8,128)S(1)}, f32[2,5,128,128]{3,2,1,0:T(8,128)S(1)}, u32[]{:S(2)}, u32[]{:S(2)}) collective-permute-start(f32[2,5,128,128]{3,2,1,0:T(8,128)S(1)} %get-tuple-element.30), channel_id=1, source_target_pairs={{2,4},{4,2},{6,8},{8,6},{10,12},{12,10},{14,16},{16,14},{18,20},{2... | collective-permute-start | bytes 1966088 | tf_op jit(solution)/shard_map/ppermute | solution.py:593
  55.4 2.9 %copy-start.3 = (f32[2,32,128,128]{3,2,1,0:T(8,128)S(1)}, f32[2,32,128,128]{3,2,1,0:T(8,128)}, u32[]{:S(2)}) copy-start(f32[2,32,128,128]{3,2,1,0:T(8,128)} %source_ref.3) | copy-start | bytes 12582916
  55.4 2.9 %copy-start.9 = (f32[16,8]{1,0:T(8,128)S(1)}, f32[16,8]{1,0:T(8,128)}, u32[]{:S(2)}) copy-start(f32[16,8]{1,0:T(8,128)} %copy-done.8) | copy-start | bytes 1540
  55.4 2.9 %collective-permute-start.7 = (f32[2,8,128,128]{3,2,1,0:T(8,128)S(1)}, f32[2,8,128,128]{3,2,1,0:T(8,128)S(1)}, u32[]{:S(2)}, u32[]{:S(2)}) collective-permute-start(f32[2,8,128,128]{3,2,1,0:T(8,128)S(1)} %get-tuple-element.34), channel_id=1, source_target_pairs={{0,2},{2,0},{4,6},{6,4},{8,10},{10,8},{12,14},{14,12},{16,18},{18,... | collective-permute-start | bytes 3145736 | tf_op jit(solution)/shard_map/ppermute | solution.py:592
